TPU v7x, 32 devices: a whole 2x2x4 slice. The times are simulated.
32 devices in a mesh: row: 4 (over y, core), col: 8 (over z, x).
Axes of the slice: x: 2, y: 2, z: 4, core: 2. Of those that a mesh axis runs over, the one named last changes fastest.
Arguments:
- inverse_block: bfloat16 [4096, 4096], P('row', 'col'), may hold values from -0.75 to 0.75
- tile_mask: int32 [32, 32], P('row', 'col'), may hold values 0 or 1
- factor: bfloat16 [2, 4096, 256], P(None, 'row'), may hold values from -0.29882812 to 0.29882812
- panel_mask: int32 [2, 32], P(None, 'row'), may hold values 0 or 1
- child_top: bfloat16 [256, 256], replicated, may hold values from -0.375 to 0.375
- pivots: float32 [2, 256, 256], replicated, may hold values from -6 to 6
Outputs:
- parent_column: float32 [4096, 256], P(('row', 'col'))
- parent_diag: float32 [256, 256], replicated
- child_upper: float32 [256, 256], replicated
- child_column: float32 [4096, 256], P(('row', 'col'))
- child_diag: float32 [256, 256], replicated
All inputs are finite; a program needn't handle non-finite values. No bound on the sum of `tile_mask` or of `panel_mask` on one device may be relied on, other than what follows from the above.
Results may differ from a plain program's by a relative error of at most 0.0003.
Values may be sent and summed in bfloat16 or wider, within the bound.
A program may use at most 64 MiB of HBM per device.

v0:
```python
import jax
import jax.numpy as jnp
from jax import lax
from jax.sharding import PartitionSpec as P


def broadcast(value, axis, source):
    kept = jnp.where(lax.axis_index(axis) == source, value, 0).astype(value.dtype)
    return lax.psum(kept, axis)


def shards(inverse_block, tile_mask, factor, panel_mask, child_top, pivots):
    tile_rows, tile_cols = inverse_block.shape
    panel_width = factor.shape[2]
    ncols = lax.axis_size("col")
    ratio = ncols // lax.axis_size("row")
    col_index = lax.axis_index("col")
    root_row = col_index // ratio
    half_index = col_index % ratio
    keep_rows = tile_rows // ncols
    highest = lax.Precision.HIGHEST
    top_float = child_top.astype(jnp.float32)
    mask_factor = tile_mask.astype(jnp.bfloat16)[:, None, :, None]
    masked = (
        inverse_block.reshape(tile_rows // 128, 128, tile_cols // 128, 128) * mask_factor
    ).reshape(tile_rows, tile_cols)
    keep_panel = panel_mask.astype(jnp.bfloat16)
    panels = (
        factor.reshape(2, tile_rows // 128, 128, panel_width) * keep_panel[:, :, None, None]
    ).reshape(2, tile_rows, panel_width)
    arrived = broadcast(panels, "row", root_row)
    received = lax.dynamic_slice_in_dim(arrived, half_index * tile_cols, tile_cols, 1)
    joined_panels = jnp.concatenate([received[0], received[1]], axis=1)
    summed = lax.psum_scatter(
        jnp.dot(masked, joined_panels, preferred_element_type=jnp.float32),
        "col",
        scatter_dimension=0,
        tiled=True,
    )
    parent_sum = summed[:, :panel_width]
    child_sum = summed[:, panel_width:]
    parent_column = -parent_sum
    child_column = -(jnp.dot(parent_column, top_float, precision=highest) + child_sum)
    own_rows = lax.dynamic_slice_in_dim(panels, col_index * keep_rows, keep_rows, 1).astype(
        jnp.float32
    )
    pivot_term = jnp.dot(own_rows[0].T, parent_column, precision=highest)
    upper_term = jnp.dot(parent_column.T, own_rows[1], precision=highest)
    pivot_sum, upper_sum = lax.psum((pivot_term, upper_term), ("row", "col"))
    parent_diag = pivots[0] - pivot_sum
    child_upper = -(jnp.dot(parent_diag, top_float, precision=highest) + upper_sum)
    child_pivot_term = jnp.dot(own_rows[1].T, child_column, precision=highest)
    child_sum_total = lax.psum(child_pivot_term, ("row", "col"))
    child_diag = pivots[1] - jnp.dot(top_float.T, child_upper, precision=highest) - child_sum_total
    return (parent_column, parent_diag, child_upper, child_column, child_diag)


def solution(mesh):
    in_specs = (P("row", "col"), P("row", "col"), P(None, "row", None), P(None, "row"), P(), P())
    out_specs = (P(("row", "col"), None), P(), P(), P(("row", "col"), None), P())
    return jax.shard_map(shards, mesh=mesh, in_specs=in_specs, out_specs=out_specs, check_vma=False)
```

profile of v0, /device:TPU:0, one launch (start us, length us, event | category | flops | bytes accessed | tf_op | source)
XLA Modules:
  0.0 268.9 jit_solution(16819982054190205230)
XLA Ops:
  7.2 0.0 copy-start
  7.2 0.0 all-reduce.4.cloned.1.call-start
  7.2 0.7 convert_element_type.11
  7.9 0.1 broadcast_bitcast_fusion
  8.0 2.6 broadcast_select_fusion
  10.6 0.0 all-reduce.4.cloned.1.call-update
  10.6 0.0 reduce-scatter.2.cloned.1.call-start
  10.7 0.1 copy.11
  10.8 38.7 %all-reduce.4.cloned.1.call-done = bf16[2,1024,256]{2,1,0:T(8,128)(2,1)} async-done(((bf16[2,1024,256]{2,1,0:T(8,128)(2,1)}), bf16[2,1024,256]{2,1,0:T(8,128)(2,1)}) %all-reduce.4.cloned.1.call-update) | async-done | bytes 1048592 | tf_op jit(solution)/shard_map/psum | solution.py:9
  49.5 1.1 dynamic-slice_bitcast_fusion.1
  50.6 0.3 mul.30
  51.0 2.1 fusion.4
  53.0 0.0 reduce-scatter.2.cloned.1.call-update
  53.0 0.0 slice-start
  53.1 0.0 all-reduce.6.cloned.1.call-start
  53.1 68.4 %reduce-scatter.2.cloned.1.call-done = f32[128,512]{1,0:T(8,128)} async-done(((f32[1024,512]{1,0:T(8,128)}), f32[128,512]{1,0:T(8,128)}) %reduce-scatter.2.cloned.1.call-update) | async-done | bytes 262160 | tf_op jit(solution)/shard_map/reduce_scatter | solution.py:34
  121.5 0.9 slice_negate_fusion
  122.4 0.0 copy-start.1
  122.4 1.0 fusion.11
  123.5 1.0 fusion.9
  124.5 1.1 fusion.3
  125.6 0.0 copy-start.6
  125.6 1.0 fusion.10
  126.7 0.0 all-reduce.6.cloned.1.call-update
  126.7 0.1 copy.16
  126.8 130.9 %all-reduce.6.cloned.1.call-done = (f32[256,256]{1,0:T(8,128)}, f32[256,256]{1,0:T(8,128)}, f32[256,256]{0,1:T(8,128)}) async-done(((f32[256,256]{1,0:T(8,128)}, f32[256,256]{1,0:T(8,128)}, f32[256,256]{0,1:T(8,128)}), (f32[256,256]{1,0:T(8,128)}, f32[256,256]{1,0:T(8,128)}, f32[256,256]{0,1:T(8,128)})) %all-reduce.6.cloned.1.call-update) | async-done | bytes 786448 | tf_op jit(solution)/shard_map/psum | solution.py:49
  257.8 1.0 bitcast_subtract_fusion
  258.8 0.0 copy-start.2
  258.8 1.3 fusion.2
  260.1 0.0 copy-start.3
  260.1 1.4 fusion.1
  261.6 0.8 copy.14
  (14 shorter events, 0.0 us)
Async XLA Ops:
  7.2 117.3 %copy-start = (bf16[256,256]{1,0:T(8,128)(2,1)S(1)}, bf16[256,256]{1,0:T(8,128)(2,1)}, u32[]{:S(2)}) copy-start(bf16[256,256]{1,0:T(8,128)(2,1)} %param.10) | copy-start | bytes 393220
  7.2 42.4 %all-reduce.4.cloned.1.call-start = ((), (), s32[]{:S(2)}) async-start(), calls=%async_computation.1 | async-start | bytes 2097152 | tf_op jit(solution)/shard_map/psum | solution.py:9
  8.0 2.7 copy-start.7
  10.6 40.4 %copy-start.5 = (bf16[1024,512]{1,0:T(8,128)(2,1)S(1)}, bf16[1024,512]{1,0:T(8,128)(2,1)}, u32[]{:S(2)}) copy-start(bf16[1024,512]{1,0:T(8,128)(2,1)} %param.6) | copy-start | bytes 3145732
  10.6 110.9 %reduce-scatter.2.cloned.1.call-start = ((), (), s32[]{:S(2)}) async-start(), calls=%async_computation.2 | async-start | bytes 2359296 | tf_op jit(solution)/shard_map/reduce_scatter | solution.py:34
  53.0 73.7 %slice-start = ((f32[2,256,256]{2,1,0:T(8,128)}), f32[1,256,256]{2,1,0:T(8,128)S(1)}, s32[]{:S(2)}) async-start(f32[2,256,256]{2,1,0:T(8,128)} %param.11), calls=%async_computation.4 | async-start | bytes 524288 | tf_op jit(solution)/shard_map/slice | solution.py:54
  53.0 204.7 %copy-start.4 = (f32[2,256,256]{2,1,0:T(8,128)S(1)}, f32[2,256,256]{2,1,0:T(8,128)}, u32[]{:S(2)}) copy-start(f32[2,256,256]{2,1,0:T(8,128)} %param.11) | copy-start | bytes 1572868
  53.1 204.7 %all-reduce.6.cloned.1.call-start = ((), (), s32[]{:S(2)}) async-start(), calls=%async_computation.3 | async-start | bytes 1572864 | tf_op jit(solution)/shard_map/psum | solution.py:49
  122.4 136.3 %copy-start.1 = (f32[128,256]{1,0:T(8,128)}, f32[128,256]{1,0:T(8,128)S(1)}, u32[]{:S(2)}) copy-start(f32[128,256]{1,0:T(8,128)S(1)} %slice_negate_fusion) | copy-start | bytes 393220
  125.6 135.9 %copy-start.6 = (f32[128,256]{1,0:T(8,128)}, f32[128,256]{1,0:T(8,128)S(1)}, u32[]{:S(2)}) copy-start(f32[128,256]{1,0:T(8,128)S(1)} %fusion.3) | copy-start | bytes 393220
  258.8 3.6 %copy-start.2 = (f32[256,256]{1,0:T(8,128)}, f32[256,256]{1,0:T(8,128)S(1)}, u32[]{:S(2)}) copy-start(f32[256,256]{1,0:T(8,128)S(1)} %bitcast_subtract_fusion) | copy-start | bytes 786436
  260.1 2.3 copy-start.3
Sparse Core Ops, SparseCore 0:
  10.7 38.7 all-reduce.3
  53.5 67.9 reduce-scatter.1
  128.5 129.1 all-reduce.5
where the time goes:
time: 269 us
  waiting for transfers between devices  238 us (88%)
  between operations  13.9 us (5%)
  matrix products  9 us (3%)
  other arithmetic  5.16 us (2%)
    psum x1, waiting for transfers between devices, shards(): pivot_sum, upper_sum = lax.psum((pivot_term, upper_term), ('row', 'col'))  131 us
    reduce_scatter x1, waiting for transfers between devices, shards(): lax.psum_scatter(jnp.dot(masked, joined_panels, preferred_element_type=jn...  68.4 us
    psum x1, waiting for transfers between devices, broadcast(): return lax.psum(kept, axis)  38.7 us
  transfers between devices with their start and end apart: 3, of which 3 were waited for; matrix products, arithmetic and copies ran while one was open for 0% of the time, Pallas kernels for 0%

commit v1 on v0

v1 whole, which is shorter than its diff:
```python
import functools

import jax
import jax.numpy as jnp
from jax import lax
from jax.experimental import pallas as pl
from jax.experimental.pallas import tpu as pltpu
from jax.sharding import PartitionSpec as P

BLOCK = 128
MESH = pl.DeviceIdType.MESH
F32 = jnp.float32
BF16 = jnp.bfloat16


def split(a):
    high = a.astype(BF16)
    return high, (a - high.astype(F32)).astype(BF16)


def dot(a, b):
    return jnp.dot(a, b, preferred_element_type=F32)


def dot_t(a, b):
    return lax.dot_general(a, b, (((0,), (0,)), ((), ())), preferred_element_type=F32)


def kernel(
    nr, nc, m_ref, tm_ref, f_ref, pm_ref, top_ref, piv_ref,
    pc_ref, pd_ref, cu_ref, cc_ref, cd_ref,
    mk, jown, jz, mx, q, zs, zr, gp, gr, gc, gown, gfull,
    ps_sem, pr_sem, fs_sem, ms_sem, mr_sem, zs_sem, zr_sem,
    as_sem, ar_sem, bs_sem, br_sem, cs_sem, cr_sem, ds_sem, dr_sem,
):
    r, c = lax.axis_index("row"), lax.axis_index("col")
    ratio = nc // nr
    rows, cols = m_ref.shape
    width = f_ref.shape[2]
    kr = rows // nc
    qr = cols // 2
    grows = gp.shape[0] // nr
    gcols = gown.shape[0]
    shared = gc.shape[0] == nc
    x, z = lax.rem(c, ratio), lax.div(c, ratio)
    chip, core = lax.div(r, 2), lax.rem(r, 2)
    chips = nr // 2
    mate = chip * 2 + 1 - core
    is_source = r == z
    same_chip = chip == lax.div(z, 2)
    sent = []

    def copy(src, dst, send, recv, row, col):
        return pltpu.make_async_remote_copy(
            src_ref=src, dst_ref=dst, send_sem=send, recv_sem=recv,
            device_id=(row, col), device_id_type=MESH,
        )

    def start(src, dst, send, recv, row, col):
        made = copy(src, dst, send, recv, row, col)
        made.start()
        sent.append(made)

    def arrived(dst, send, recv):
        copy(dst, dst, send, recv, r, c).wait_recv()

    def at(ref, first, count):
        return ref.at[pl.ds(pl.multiple_of(first, 16), count)]

    barrier = pltpu.get_barrier_semaphore()
    for d in range(1, nr):
        pl.semaphore_signal(
            barrier, inc=1, device_id=(lax.rem(r + d, nr), c), device_id_type=MESH
        )
    for d in range(1, nc):
        pl.semaphore_signal(
            barrier, inc=1, device_id=(r, lax.rem(c + d, nc)), device_id_type=MESH
        )
    for b in range(rows // BLOCK):
        part = slice(b * BLOCK, (b + 1) * BLOCK)
        for s in range(2):
            keep = pm_ref[s, b].astype(F32)
            jown[part, s * width : (s + 1) * width] = (f_ref[s, part, :].astype(F32) * keep).astype(BF16)
    pl.semaphore_wait(barrier, nr + nc - 2)

    def piece(ref, e, h):
        half = lax.rem(x + e, ratio)
        return at(ref, (half * 2 + h) * qr, qr)

    def panel_copies(e):
        made = []
        for h in range(2):
            i = 2 * e + h
            made.append(
                copy(piece(jown, e, h), piece(jz, e, h), ps_sem.at[i, 0], pr_sem.at[i], mate, c)
            )
            for d in range(1, chips):
                to = lax.rem(chip + d, chips) * 2 + h
                made.append(
                    copy(piece(jown, e, h), piece(jz, e, h), ps_sem.at[i, d], pr_sem.at[i], to, c)
                )
        return made

    def forward_copy(e):
        half = lax.rem(x + e, ratio)
        part = at(jz, (half * 2 + core) * qr, qr)
        i = 2 * e + core
        return part, copy(part, part, fs_sem.at[e], pr_sem.at[i], mate, c)

    def panels_arrive(e):
        @pl.when(jnp.logical_and(jnp.logical_not(is_source), same_chip))
        def _():
            for h in range(2):
                arrived(piece(jz, e, h), ps_sem.at[2 * e + h, 0], pr_sem.at[2 * e + h])

        @pl.when(jnp.logical_not(same_chip))
        def _():
            part, made = forward_copy(e)
            arrived(part, fs_sem.at[e], pr_sem.at[2 * e + core])
            made.start()
            half = lax.rem(x + e, ratio)
            other = at(jz, (half * 2 + 1 - core) * qr, qr)
            arrived(other, fs_sem.at[e], pr_sem.at[2 * e + 1 - core])

    @pl.when(is_source)
    def _():
        for made in panel_copies(0):
            made.start()
        jz[...] = jown[...]

    for b in range(rows // BLOCK):
        for j in range(cols // BLOCK):
            tile = (slice(b * BLOCK, (b + 1) * BLOCK), slice(j * BLOCK, (j + 1) * BLOCK))
            mk[tile] = (m_ref[tile].astype(F32) * tm_ref[b, j].astype(F32)).astype(BF16)
    for e in range(nr):
        g = lax.rem(z + 1 + e, nr)
        for d in range(1, ratio):
            xx = lax.rem(x + d, ratio)
            start(
                at(mk, (g * ratio + xx) * kr, kr), mx.at[d - 1, e],
                ms_sem.at[d - 1, e], mr_sem.at[d - 1, e], r, z * ratio + xx,
            )

    panels_arrive(0)
    near = jz[pl.ds(pl.multiple_of(x * cols, cols), cols), :]
    step = min(rows, 256)
    for b in range(rows // step):
        part = slice(b * step, (b + 1) * step)
        q[part, :] = dot(mk[part, :], near)

    @pl.when(is_source)
    def _():
        for e in range(1, ratio):
            for made in panel_copies(e):
                made.start()

    for j in range(2 * width // BLOCK):
        left = 0 if j * BLOCK < width else width
        high, low = split(q[:, j * BLOCK : (j + 1) * BLOCK])
        own = jown[:, left:]
        value = dot_t(own, high) + dot_t(own, low)
        slots = width // BLOCK
        if left == 0:
            gp[j * width : (j + 1) * width, :] = value[:width]
            gp[(slots + j) * width : (slots + j + 1) * width, :] = value[width:]
        else:
            gp[(slots + j) * width : (slots + j + 1) * width, :] = value
    for d in range(1, nr):
        to = lax.rem(r + d, nr)
        start(at(gp, to * grows, grows), gr.at[d - 1], as_sem.at[d - 1], ar_sem.at[d - 1], to, c)
    total = gp[pl.ds(pl.multiple_of(r * grows, 16), grows), :]
    for d in range(1, nr):
        arrived(gr.at[d - 1], as_sem.at[d - 1], ar_sem.at[d - 1])
        total = total + gr[d - 1]
    if shared:
        gc[pl.ds(c, 1)] = total[None]
        for d in range(1, nc):
            to = lax.rem(c + d, nc)
            start(gc.at[c], gc.at[c], bs_sem.at[d - 1], br_sem.at[d - 1], r, to)
    else:
        gr[nr - 1] = total
        for d in range(1, nc):
            to = lax.rem(c + d, nc)
            start(
                gr.at[nr - 1, pl.ds(pl.multiple_of(to * gcols, 16), gcols)], gc.at[d - 1],
                bs_sem.at[d - 1], br_sem.at[d - 1], r, to,
            )

    for e in range(1, ratio):
        panels_arrive(e)
    for e in range(nr):
        g = lax.rem(z + 1 + e, nr)
        value = q[pl.ds(pl.multiple_of((g * ratio + x) * kr, 16), kr), :]
        for d in range(1, ratio):
            arrived(mx.at[d - 1, e], ms_sem.at[d - 1, e], mr_sem.at[d - 1, e])
            half = lax.rem(x - d + ratio, ratio)
            value = value + dot(mx[d - 1, e], jz[pl.ds(pl.multiple_of(half * cols, cols), cols), :])
        zs[e] = value
        if e < nr - 1:
            start(zs.at[e], zr.at[e], zs_sem.at[e], zr_sem.at[e], r, g * ratio + x)

    if shared:
        for d in range(1, nc):
            come = lax.rem(c - d + nc, nc)
            arrived(gc.at[come], bs_sem.at[d - 1], br_sem.at[d - 1])
        total = gc[0]
        for i in range(1, nc):
            total = total + gc[i]
        gfull[pl.ds(pl.multiple_of(r * grows, 16), grows), :] = total
    else:
        total = gr[nr - 1, pl.ds(pl.multiple_of(c * gcols, 16), gcols), :]
        for d in range(1, nc):
            arrived(gc.at[d - 1], bs_sem.at[d - 1], br_sem.at[d - 1])
            total = total + gc[d - 1]
        mine = r * grows + c * gcols
        gfull[pl.ds(pl.multiple_of(mine, 16), gcols), :] = total
        for d in range(1, nc):
            to = lax.rem(c + d, nc)
            start(
                at(gfull, mine, gcols), at(gfull, mine, gcols),
                cs_sem.at[d - 1], cr_sem.at[d - 1], r, to,
            )
        for d in range(1, nc):
            come = lax.rem(c - d + nc, nc)
            arrived(at(gfull, r * grows + come * gcols, gcols), cs_sem.at[d - 1], cr_sem.at[d - 1])
    for d in range(1, nr):
        to = lax.rem(r + d, nr)
        block = at(gfull, r * grows, grows)
        start(block, block, ds_sem.at[d - 1], dr_sem.at[d - 1], to, c)

    top = top_ref[...]
    value = zs[nr - 1]
    for e in range(nr - 1):
        arrived(zr.at[e], zs_sem.at[e], zr_sem.at[e])
        value = value + zr[e]
    parent = value[:, :width]
    high, low = split(parent)
    pc_ref[...] = -parent
    cc_ref[...] = dot(high, top) + dot(low, top) - value[:, width:]

    for d in range(1, nr):
        come = lax.rem(r - d + nr, nr)
        arrived(at(gfull, come * grows, grows), ds_sem.at[d - 1], dr_sem.at[d - 1])
    slots = width // BLOCK

    def square(i):
        return jnp.concatenate(
            [gfull[(i * slots + j) * width : (i * slots + j + 1) * width, :] for j in range(slots)], axis=1
        )

    diag = piv_ref[0] + square(0)
    pd_ref[...] = diag
    cross = square(1)
    high, low = split(diag)
    upper = cross.T - (dot(high, top) + dot(low, top))
    cu_ref[...] = upper
    high, low = split(upper)
    cross_high, cross_low = split(cross)
    cd_ref[...] = (
        piv_ref[1] - (dot_t(top, high) + dot_t(top, low))
        - (dot(cross_high, top) + dot(cross_low, top)) + square(2)
    )

    for made in sent:
        made.wait_send()

    @pl.when(is_source)
    def _():
        for e in range(ratio):
            for made in panel_copies(e):
                made.wait_send()

    @pl.when(jnp.logical_not(same_chip))
    def _():
        for e in range(ratio):
            forward_copy(e)[1].wait_send()


def shards(nr, nc, inverse_block, tile_mask, factor, panel_mask, child_top, pivots):
    rows, cols = inverse_block.shape
    width = factor.shape[2]
    ratio = nc // nr
    kr = rows // nc
    small = 3 * width * width // BLOCK
    grows = small // nr
    shared = grows % (16 * nc) != 0
    gcols = 16 if shared else grows // nc
    dma = pltpu.SemaphoreType.DMA
    vmem, smem = pl.BlockSpec(memory_space=pltpu.VMEM), pl.BlockSpec(memory_space=pltpu.SMEM)
    square = jax.ShapeDtypeStruct((width, width), F32)
    column = jax.ShapeDtypeStruct((kr, width), F32)
    return pl.pallas_call(
        functools.partial(kernel, nr, nc),
        out_shape=(column, square, square, column, square),
        in_specs=[vmem, smem, vmem, smem, vmem, vmem],
        out_specs=(vmem,) * 5,
        scratch_shapes=[
            pltpu.VMEM((rows, cols), BF16),
            pltpu.VMEM((rows, 2 * width), BF16),
            pltpu.VMEM((rows, 2 * width), BF16),
            pltpu.VMEM((max(ratio - 1, 1), nr, kr, cols), BF16),
            pltpu.VMEM((rows, 2 * width), F32),
            pltpu.VMEM((nr, kr, 2 * width), F32),
            pltpu.VMEM((nr - 1, kr, 2 * width), F32),
            pltpu.VMEM((small, BLOCK), F32),
            pltpu.VMEM((nr, grows, BLOCK), F32),
            pltpu.VMEM((nc, grows, BLOCK) if shared else (nc - 1, gcols, BLOCK), F32),
            pltpu.VMEM((gcols, BLOCK), F32),
            pltpu.VMEM((small, BLOCK), F32),
            dma((2 * ratio, max(nr // 2, 1))), dma((2 * ratio,)), dma((ratio,)),
            dma((max(ratio - 1, 1), nr)), dma((max(ratio - 1, 1), nr)),
            dma((nr - 1,)), dma((nr - 1,)),
            dma((nr - 1,)), dma((nr - 1,)),
            dma((nc - 1,)), dma((nc - 1,)),
            dma((nc - 1,)), dma((nc - 1,)),
            dma((nr - 1,)), dma((nr - 1,)),
        ],
        compiler_params=pltpu.CompilerParams(
            collective_id=0, has_side_effects=True, vmem_limit_bytes=40 * 1024 * 1024
        ),
    )(inverse_block, tile_mask, factor, panel_mask, child_top, pivots)


def solution(mesh):
    in_specs = (P("row", "col"), P("row", "col"), P(None, "row", None), P(None, "row"), P(), P())
    out_specs = (P(("row", "col"), None), P(), P(), P(("row", "col"), None), P())
    body = functools.partial(shards, mesh.shape["row"], mesh.shape["col"])
    return jax.shard_map(body, mesh=mesh, in_specs=in_specs, out_specs=out_specs, check_vma=False)
```

time: 269 us -> 78.5 us (0.29)
  the two profiles are of different devices: /device:TPU:0 before, /device:TPU:1 now
where the time goes in v1:
time: 78.5 us; the launch traced here: 78.2 us
  Pallas kernels  69 us (88%)
  local copies, waits for them, and re-layouts  8.58 us (11%)
    pallas_call x1, Pallas kernels, shards(): pl.pallas_call(functools.partial(kernel, nr, nc), out_shape=(column, squa...  69 us
    unnamed x16, local copies, waits for them, and re-layouts  8.58 us

profile of v1, /device:TPU:1, one launch (start us, length us, event | category | flops | bytes accessed | tf_op | source)
XLA Modules:
  0.0 78.2 jit_solution(2520707282538978426)
XLA Ops:
  0.6 0.0 copy-start.4
  0.6 0.8 copy.11.tm_ref
  1.4 0.0 copy-done.4
  1.4 0.0 copy-start
  1.4 1.2 %copy-done = bf16[1024,512]{1,0:T(8,128)(2,1)S(1)} copy-done((bf16[1024,512]{1,0:T(8,128)(2,1)S(1)}, bf16[1024,512]{1,0:T(8,128)(2,1)}, u32[]{:S(2)}) %copy-start) | copy-done | bytes 1048600
  2.6 0.0 copy-start.1
  2.6 1.2 %copy-done.1 = bf16[2,1024,256]{2,1,0:T(8,128)(2,1)S(1)} copy-done((bf16[2,1024,256]{2,1,0:T(8,128)(2,1)S(1)}, bf16[2,1024,256]{2,1,0:T(8,128)(2,1)}, u32[]{:S(2)}) %copy-start.1) | copy-done | bytes 1048600
  3.9 0.0 copy-start.2
  3.9 1.0 %copy-done.2 = f32[2,256,256]{2,1,0:T(8,128)S(1)} copy-done((f32[2,256,256]{2,1,0:T(8,128)S(1)}, f32[2,256,256]{2,1,0:T(8,128)}, u32[]{:S(2)}) %copy-start.2) | copy-done | bytes 524312
  4.9 0.0 copy-start.3
  4.9 0.9 %copy-done.3 = bf16[256,256]{1,0:T(8,128)(2,1)S(1)} copy-done((bf16[256,256]{1,0:T(8,128)(2,1)S(1)}, bf16[256,256]{1,0:T(8,128)(2,1)}, u32[]{:S(2)}) %copy-start.3) | copy-done | bytes 131096
  5.8 69.0 %shard_map.101 = (f32[128,256]{1,0:T(8,128)S(1)}, f32[256,256]{1,0:T(8,128)S(1)}, f32[256,256]{1,0:T(8,128)S(1)}, f32[128,256]{1,0:T(8,128)S(1)}, f32[256,256]{1,0:T(8,128)S(1)}) custom-call(bf16[1024,512]{1,0:T(8,128)(2,1)S(1)} %copy-done, s32[8,4]{1,0:T(8,128)S(1)} %copy.11.tm_ref, bf16[2,1024,256]{2,1,0:T(8,128)(2,1)S(1)} %copy-done.1, ...), custom_call_target="tpu_custom_call" | custom-call | tf_op jit(solution)/shard_map/pallas_call | solution.py:292
  74.8 0.7 copy.17
  75.4 0.7 copy.18
  76.1 0.7 copy.19
  76.8 0.7 copy.20
  77.5 0.7 copy.21
Async XLA Ops:
  0.6 0.8 copy-start.4
  1.4 1.2 %copy-start = (bf16[1024,512]{1,0:T(8,128)(2,1)S(1)}, bf16[1024,512]{1,0:T(8,128)(2,1)}, u32[]{:S(2)}) copy-start(bf16[1024,512]{1,0:T(8,128)(2,1)} %m_ref.1) | copy-start | bytes 3145732
  2.6 1.2 %copy-start.1 = (bf16[2,1024,256]{2,1,0:T(8,128)(2,1)S(1)}, bf16[2,1024,256]{2,1,0:T(8,128)(2,1)}, u32[]{:S(2)}) copy-start(bf16[2,1024,256]{2,1,0:T(8,128)(2,1)} %f_ref.1) | copy-start | bytes 3145732
  3.9 1.0 %copy-start.2 = (f32[2,256,256]{2,1,0:T(8,128)S(1)}, f32[2,256,256]{2,1,0:T(8,128)}, u32[]{:S(2)}) copy-start(f32[2,256,256]{2,1,0:T(8,128)} %piv_ref.1) | copy-start | bytes 1572868
  4.9 0.9 %copy-start.3 = (bf16[256,256]{1,0:T(8,128)(2,1)S(1)}, bf16[256,256]{1,0:T(8,128)(2,1)}, u32[]{:S(2)}) copy-start(bf16[256,256]{1,0:T(8,128)(2,1)} %top_ref.1) | copy-start | bytes 393220

commit v2 on v1

v2 whole, which is shorter than its diff:
```python
import functools

import jax
import jax.numpy as jnp
from jax import lax
from jax.experimental import pallas as pl
from jax.experimental.pallas import tpu as pltpu
from jax.sharding import PartitionSpec as P

BLOCK = 128
GROUP = 16
MESH = pl.DeviceIdType.MESH
F32 = jnp.float32
BF16 = jnp.bfloat16


def split(a):
    high = a.astype(BF16)
    return high, (a - high.astype(F32)).astype(BF16)


def dot(a, b):
    return jnp.dot(a, b, preferred_element_type=F32)


def dot_t(a, b):
    return lax.dot_general(a, b, (((0,), (0,)), ((), ())), preferred_element_type=F32)


def quantize(a):
    groups = a.shape[0] // GROUP
    parts = a.reshape(groups, GROUP, a.shape[1])
    largest = jnp.maximum(jnp.max(jnp.abs(parts), axis=1), 1e-30)
    whole = jnp.round(parts * (32767.0 / largest)[:, None, :]).astype(jnp.int32)
    return whole.reshape(a.shape).astype(jnp.int16), largest * (1.0 / 32767.0)


def restore(whole, scale):
    groups = whole.shape[0] // GROUP
    parts = whole.astype(jnp.int32).astype(F32).reshape(groups, GROUP, whole.shape[1])
    return (parts * scale[:groups][:, None, :]).reshape(whole.shape)


def kernel(
    nr, nc, m_any, tm_any, f_any, pm_any, sum_ref, g_ref,
    m_ref, tm_ref, f_ref, pm_ref, mk, jown, jt, jz, mx, q, own, zq, zx, zrq, zrx, gp,
    gpq, gps, grq, grs, gtq, gts, gcq, gcs, gfq, gfs, in_sem,
    ps_sem, pr_sem, fs_sem, ms_sem, mr_sem, zs_sem, zr_sem,
    as_sem, ar_sem, bs_sem, br_sem, cs_sem, cr_sem, ds_sem, dr_sem,
):
    r, c = lax.axis_index("row"), lax.axis_index("col")
    ratio = nc // nr
    rows, cols = m_ref.shape
    width = f_ref.shape[2]
    kr = rows // nc
    qr = cols // 2
    grows = gp.shape[0] // nr
    lots = gfs.shape[1]
    shared = lots == 1
    gcols = grows // lots
    x, z = lax.rem(c, ratio), lax.div(c, ratio)
    chip, core = lax.div(r, 2), lax.rem(r, 2)
    chips = nr // 2
    mate = chip * 2 + 1 - core
    is_source = r == z
    same_chip = chip == lax.div(z, 2)
    sent = []

    loads = [
        pltpu.make_async_copy(there, here, in_sem.at[i])
        for i, (there, here) in enumerate(
            ((pm_any, pm_ref), (f_any, f_ref), (tm_any, tm_ref), (m_any, m_ref))
        )
    ]
    for load in loads:
        load.start()

    def copy(src, dst, send, recv, row, col):
        return pltpu.make_async_remote_copy(
            src_ref=src, dst_ref=dst, send_sem=send, recv_sem=recv,
            device_id=(row, col), device_id_type=MESH,
        )

    def start(src, dst, send, recv, row, col):
        made = copy(src, dst, send, recv, row, col)
        made.start()
        sent.append(made)

    def arrived(dst, send, recv):
        copy(dst, dst, send, recv, r, c).wait_recv()

    def at(ref, first, count):
        return ref.at[pl.ds(pl.multiple_of(first, 16), count)]

    barrier = pltpu.get_barrier_semaphore()
    for d in range(1, nr):
        pl.semaphore_signal(
            barrier, inc=1, device_id=(lax.rem(r + d, nr), c), device_id_type=MESH
        )
    for d in range(1, nc):
        pl.semaphore_signal(
            barrier, inc=1, device_id=(r, lax.rem(c + d, nc)), device_id_type=MESH
        )
    loads[0].wait()
    loads[1].wait()
    for b in range(rows // BLOCK):
        part = slice(b * BLOCK, (b + 1) * BLOCK)
        for s in range(2):
            keep = pm_ref[s : s + 1, b : b + 1].astype(F32)
            jown[part, s * width : (s + 1) * width] = (f_ref[s, part, :].astype(F32) * keep).astype(BF16)
    pl.semaphore_wait(barrier, nr + nc - 2)

    def piece(ref, e, h):
        half = lax.rem(x + e, ratio)
        return at(ref, (half * 2 + h) * qr, qr)

    def panel_copies(e):
        made = []
        for h in range(2):
            i = 2 * e + h
            for d in range(1, chips):
                to = lax.rem(chip + d, chips) * 2 + h
                made.append(
                    copy(piece(jown, e, h), piece(jz, e, h), ps_sem.at[i, d], pr_sem.at[i], to, c)
                )
            made.append(
                copy(piece(jown, e, h), piece(jz, e, h), ps_sem.at[i, 0], pr_sem.at[i], mate, c)
            )
        return made

    def forward_copy(e):
        half = lax.rem(x + e, ratio)
        part = at(jz, (half * 2 + core) * qr, qr)
        i = 2 * e + core
        return part, copy(part, part, fs_sem.at[e], pr_sem.at[i], mate, c)

    def panels_arrive(e):
        @pl.when(jnp.logical_and(jnp.logical_not(is_source), same_chip))
        def _():
            for h in range(2):
                arrived(piece(jz, e, h), ps_sem.at[2 * e + h, 0], pr_sem.at[2 * e + h])

        @pl.when(jnp.logical_not(same_chip))
        def _():
            part, made = forward_copy(e)
            arrived(part, fs_sem.at[e], pr_sem.at[2 * e + core])
            made.start()
            half = lax.rem(x + e, ratio)
            other = at(jz, (half * 2 + 1 - core) * qr, qr)
            arrived(other, fs_sem.at[e], pr_sem.at[2 * e + 1 - core])

    @pl.when(is_source)
    def _():
        for made in panel_copies(0):
            made.start()

    loads[2].wait()
    loads[3].wait()
    for b in range(rows // BLOCK):
        for j in range(cols // BLOCK):
            tile = (slice(b * BLOCK, (b + 1) * BLOCK), slice(j * BLOCK, (j + 1) * BLOCK))
            keep = tm_ref[b : b + 1, j : j + 1].astype(F32)
            mk[tile] = (m_ref[tile].astype(F32) * keep).astype(BF16)
    for e in range(nr):
        g = lax.rem(z + 1 + e, nr)
        for d in range(1, ratio):
            xx = lax.rem(x + d, ratio)
            start(
                at(mk, (g * ratio + xx) * kr, kr), mx.at[d - 1, e],
                ms_sem.at[d - 1, e], mr_sem.at[d - 1, e], r, z * ratio + xx,
            )

    jt[...] = jown[...].T

    @pl.when(is_source)
    def _():
        jz[...] = jown[...]
        for made in panel_copies(0):
            made.wait_send()
        for e in range(1, ratio):
            for made in panel_copies(e):
                made.start()

    panels_arrive(0)
    near = jz[pl.ds(pl.multiple_of(x * cols, cols), cols), :]
    step = min(rows, 256)
    for b in range(rows // step):
        part = slice(b * step, (b + 1) * step)
        q[part, :] = dot(mk[part, :], near)

    slots = width // BLOCK
    for s in range(2):
        high, low = split(q[:, s * width : (s + 1) * width])
        turned = jt[s * width :, :]
        value = dot(turned, high) + dot(turned, low)
        for i in range(2 - s):
            for j in range(slots):
                first = ((i + 2 * s) * slots + j) * width
                gp[first : first + width, :] = value[
                    i * width : (i + 1) * width, j * BLOCK : (j + 1) * BLOCK
                ]
    glines = grows // GROUP
    for i in range(nr):
        part = slice(i * grows, (i + 1) * grows)
        gpq[part, :], gps[i, :glines, :] = quantize(gp[part, :])
    for d in range(1, nr):
        to = lax.rem(r + d, nr)
        start(gps.at[to], grs.at[d - 1], as_sem.at[1, d - 1], ar_sem.at[1, d - 1], to, c)
        start(at(gpq, to * grows, grows), grq.at[d - 1], as_sem.at[0, d - 1], ar_sem.at[0, d - 1], to, c)
    total = gp[pl.ds(pl.multiple_of(r * grows, 16), grows), :]
    for d in range(1, nr):
        arrived(grs.at[d - 1], as_sem.at[1, d - 1], ar_sem.at[1, d - 1])
        arrived(grq.at[d - 1], as_sem.at[0, d - 1], ar_sem.at[0, d - 1])
        total = total + restore(grq[d - 1], grs[d - 1])
    gp[pl.ds(pl.multiple_of(r * grows, 16), grows), :] = total
    lines = gcols // GROUP
    for i in range(lots):
        part = slice(i * gcols, (i + 1) * gcols)
        gtq[part, :], gts[i, :lines, :] = quantize(total[part, :])
    for d in range(1, nc):
        to = lax.rem(c + d, nc)
        place = 0 if shared else to
        start(gts.at[place], gcs.at[c], bs_sem.at[1, d - 1], br_sem.at[1, d - 1], r, to)
        start(at(gtq, place * gcols, gcols), gcq.at[c], bs_sem.at[0, d - 1], br_sem.at[0, d - 1], r, to)
    place = 0 if shared else c
    gcs[pl.ds(c, 1)] = gts[pl.ds(place, 1)]
    gcq[pl.ds(c, 1)] = gtq[pl.ds(pl.multiple_of(place * gcols, 16), gcols), :][None]

    for e in range(1, ratio):
        panels_arrive(e)
    zlines = kr // GROUP
    for e in range(nr):
        g = lax.rem(z + 1 + e, nr)
        value = q[pl.ds(pl.multiple_of((g * ratio + x) * kr, 16), kr), :]
        for d in range(1, ratio):
            arrived(mx.at[d - 1, e], ms_sem.at[d - 1, e], mr_sem.at[d - 1, e])
            half = lax.rem(x - d + ratio, ratio)
            value = value + dot(mx[d - 1, e], jz[pl.ds(pl.multiple_of(half * cols, cols), cols), :])
        if e < nr - 1:
            zq[e], zx[e, :zlines, :] = quantize(value)
            to = g * ratio + x
            start(zx.at[e], zrx.at[e], zs_sem.at[1, e], zr_sem.at[1, e], r, to)
            start(zq.at[e], zrq.at[e], zs_sem.at[0, e], zr_sem.at[0, e], r, to)
        else:
            own[...] = value

    total = None
    for d in range(1, nc):
        come = lax.rem(c + nc - d, nc)
        arrived(gcs.at[come], bs_sem.at[1, d - 1], br_sem.at[1, d - 1])
        arrived(gcq.at[come], bs_sem.at[0, d - 1], br_sem.at[0, d - 1])
    for i in range(nc):
        value = restore(gcq[i], gcs[i])
        total = value if total is None else total + value
    mine = r * grows + place * gcols
    whole, scale = quantize(total)
    gfq[pl.ds(pl.multiple_of(mine, 16), gcols), :] = whole
    padding = gfs.shape[2] - lines
    if padding:
        scale = jnp.concatenate([scale, jnp.zeros((padding, BLOCK), F32)], axis=0)
    gfs[r, place] = scale
    if not shared:
        for d in range(1, nc):
            to = lax.rem(c + d, nc)
            start(gfs.at[r, c], gfs.at[r, c], cs_sem.at[1, d - 1], cr_sem.at[1, d - 1], r, to)
            block = at(gfq, mine, gcols)
            start(block, block, cs_sem.at[0, d - 1], cr_sem.at[0, d - 1], r, to)
        for d in range(1, nc):
            come = lax.rem(c + nc - d, nc)
            arrived(gfs.at[r, come], cs_sem.at[1, d - 1], cr_sem.at[1, d - 1])
            arrived(at(gfq, r * grows + come * gcols, gcols), cs_sem.at[0, d - 1], cr_sem.at[0, d - 1])
    for d in range(1, nr):
        to = lax.rem(r + d, nr)
        start(gfs.at[r], gfs.at[r], ds_sem.at[1, d - 1], dr_sem.at[1, d - 1], to, c)
        block = at(gfq, r * grows, grows)
        start(block, block, ds_sem.at[0, d - 1], dr_sem.at[0, d - 1], to, c)

    value = own[...]
    for e in range(nr - 1):
        arrived(zrx.at[e], zs_sem.at[1, e], zr_sem.at[1, e])
        arrived(zrq.at[e], zs_sem.at[0, e], zr_sem.at[0, e])
        value = value + restore(zrq[e], zrx[e])
    sum_ref[...] = value

    for d in range(1, nr):
        come = lax.rem(r + nr - d, nr)
        arrived(gfs.at[come], ds_sem.at[1, d - 1], dr_sem.at[1, d - 1])
        arrived(at(gfq, come * grows, grows), ds_sem.at[0, d - 1], dr_sem.at[0, d - 1])
    for i in range(nr):
        for j in range(lots):
            part = slice(i * grows + j * gcols, i * grows + (j + 1) * gcols)
            g_ref[part, :] = restore(gfq[part, :], gfs[i, j])

    for made in sent:
        made.wait_send()

    @pl.when(is_source)
    def _():
        for e in range(1, ratio):
            for made in panel_copies(e):
                made.wait_send()

    @pl.when(jnp.logical_not(same_chip))
    def _():
        for e in range(ratio):
            forward_copy(e)[1].wait_send()


def finish(sum_ref, g_ref, top_ref, piv_ref, pc_ref, pd_ref, cu_ref, cc_ref, cd_ref):
    width = top_ref.shape[0]
    slots = width // BLOCK
    top = top_ref[...]
    value = sum_ref[...]
    parent = value[:, :width]
    high, low = split(parent)
    pc_ref[...] = -parent
    cc_ref[...] = dot(high, top) + dot(low, top) - value[:, width:]

    def square(i):
        return jnp.concatenate(
            [g_ref[(i * slots + j) * width : (i * slots + j + 1) * width, :] for j in range(slots)], axis=1
        )

    diag = piv_ref[0] + square(0)
    pd_ref[...] = diag
    cross = square(1)
    high, low = split(diag)
    upper = cross.T - (dot(high, top) + dot(low, top))
    cu_ref[...] = upper
    high, low = split(upper)
    cross_high, cross_low = split(cross)
    cd_ref[...] = (
        piv_ref[1] - (dot_t(top, high) + dot_t(top, low))
        - (dot(cross_high, top) + dot(cross_low, top)) + square(2)
    )


def eights(count):
    return -(-count // 8) * 8


def shards(nr, nc, inverse_block, tile_mask, factor, panel_mask, child_top, pivots):
    rows, cols = inverse_block.shape
    width = factor.shape[2]
    ratio = nc // nr
    kr = rows // nc
    small = 3 * width * width // BLOCK
    grows = small // nr
    lots = nc if grows % (GROUP * nc) == 0 else 1
    gcols = grows // lots
    dma = pltpu.SemaphoreType.DMA
    vmem, anywhere = pl.BlockSpec(memory_space=pltpu.VMEM), pl.BlockSpec(memory_space=pl.ANY)
    square = jax.ShapeDtypeStruct((width, width), F32)
    column = jax.ShapeDtypeStruct((kr, width), F32)
    others = max(ratio - 1, 1)
    zlines, glines, clines = eights(kr // GROUP), eights(grows // GROUP), eights(gcols // GROUP)
    I16 = jnp.int16
    summed, small_sums = pl.pallas_call(
        functools.partial(kernel, nr, nc),
        out_shape=(jax.ShapeDtypeStruct((kr, 2 * width), F32), jax.ShapeDtypeStruct((small, BLOCK), F32)),
        in_specs=[anywhere] * 4,
        out_specs=(vmem,) * 2,
        scratch_shapes=[
            pltpu.VMEM(inverse_block.shape, BF16),
            pltpu.VMEM(tile_mask.shape, jnp.int32),
            pltpu.VMEM(factor.shape, BF16),
            pltpu.VMEM(panel_mask.shape, jnp.int32),
            pltpu.VMEM((rows, cols), BF16),
            pltpu.VMEM((rows, 2 * width), BF16),
            pltpu.VMEM((2 * width, rows), BF16),
            pltpu.VMEM((rows, 2 * width), BF16),
            pltpu.VMEM((others, nr, kr, cols), BF16),
            pltpu.VMEM((rows, 2 * width), F32),
            pltpu.VMEM((kr, 2 * width), F32),
            pltpu.VMEM((nr - 1, kr, 2 * width), I16),
            pltpu.VMEM((nr - 1, zlines, 2 * width), F32),
            pltpu.VMEM((nr - 1, kr, 2 * width), I16),
            pltpu.VMEM((nr - 1, zlines, 2 * width), F32),
            pltpu.VMEM((small, BLOCK), F32),
            pltpu.VMEM((small, BLOCK), I16),
            pltpu.VMEM((nr, glines, BLOCK), F32),
            pltpu.VMEM((nr - 1, grows, BLOCK), I16),
            pltpu.VMEM((nr - 1, glines, BLOCK), F32),
            pltpu.VMEM((grows, BLOCK), I16),
            pltpu.VMEM((lots, clines, BLOCK), F32),
            pltpu.VMEM((nc, gcols, BLOCK), I16),
            pltpu.VMEM((nc, clines, BLOCK), F32),
            pltpu.VMEM((small, BLOCK), I16),
            pltpu.VMEM((nr, lots, clines, BLOCK), F32),
            dma((4,)),
            dma((2 * ratio, max(nr // 2, 1))), dma((2 * ratio,)), dma((ratio,)),
            dma((others, nr)), dma((others, nr)),
            dma((2, nr - 1)), dma((2, nr - 1)),
            dma((2, nr - 1)), dma((2, nr - 1)),
            dma((2, nc - 1)), dma((2, nc - 1)),
            dma((2, nc - 1)), dma((2, nc - 1)),
            dma((2, nr - 1)), dma((2, nr - 1)),
        ],
        compiler_params=pltpu.CompilerParams(
            collective_id=0, has_side_effects=True, vmem_limit_bytes=56 * 1024 * 1024
        ),
    )(inverse_block, tile_mask, factor, panel_mask)
    return pl.pallas_call(
        finish,
        out_shape=(column, square, square, column, square),
        in_specs=[vmem] * 4,
        out_specs=(vmem,) * 5,
        compiler_params=pltpu.CompilerParams(vmem_limit_bytes=24 * 1024 * 1024),
    )(summed, small_sums, child_top, pivots)


def solution(mesh):
    in_specs = (P("row", "col"), P("row", "col"), P(None, "row", None), P(None, "row"), P(), P())
    out_specs = (P(("row", "col"), None), P(), P(), P(("row", "col"), None), P())
    body = functools.partial(shards, mesh.shape["row"], mesh.shape["col"])
    return jax.shard_map(body, mesh=mesh, in_specs=in_specs, out_specs=out_specs, check_vma=False)
```

time: 78.5 us -> 57.9 us (0.74)
  the two profiles are of different devices: /device:TPU:1 before, /device:TPU:0 now
where the time goes in v2:
time: 57.9 us; the launch traced here: 56.9 us
  Pallas kernels  52.8 us (91%)
  local copies, waits for them, and re-layouts  3.43 us (6%)
  between operations  0.67 us (1%)
    pallas_call x1, Pallas kernels, shards(): pl.pallas_call(functools.partial(kernel, nr, nc), out_shape=(jax.ShapeDty...  51.6 us
    unnamed x9, local copies, waits for them, and re-layouts  3.43 us
    pallas_call x1, Pallas kernels, shards(): pl.pallas_call(finish, out_shape=(column, square, square, column, square)...  1.27 us

profile of v2, /device:TPU:0, one launch (start us, length us, event | category | flops | bytes accessed | tf_op | source)
XLA Modules:
  0.0 56.9 jit_solution(13431644465309074227)
XLA Ops:
  0.6 1.3 %copy.11.tm_any = s32[8,4]{1,0:T(8,128)} copy(s32[8,4]{0,1:T(4,128)} %param.7) | data formatting | bytes 256 | tf_op args[1]
  2.0 0.0 copy-start.1
  2.0 0.0 copy-start.3
  2.0 51.6 %shard_map.101 = (f32[128,512]{1,0:T(8,128)}, f32[1536,128]{1,0:T(8,128)}) custom-call(bf16[1024,512]{1,0:T(8,128)(2,1)} %m_any.1, s32[8,4]{1,0:T(8,128)} %copy.11.tm_any, bf16[2,1024,256]{2,1,0:T(8,128)(2,1)} %f_any.1, s32[2,8]{1,0:T(2,128)} %pm_any.1), custom_call_target="tpu_custom_call" | custom-call | tf_op jit(solution)/shard_map/pallas_call | solution.py:358
  53.6 0.0 copy-done.1
  53.6 0.0 copy-done.3
  53.6 0.0 copy-start
  53.6 1.1 %copy-done = f32[1536,128]{1,0:T(8,128)S(1)} copy-done((f32[1536,128]{1,0:T(8,128)S(1)}, f32[1536,128]{1,0:T(8,128)}, u32[]{:S(2)}) %copy-start) | copy-done | bytes 786456
  54.7 0.0 copy-start.2
  54.7 0.9 %copy-done.2 = f32[128,512]{1,0:T(8,128)S(1)} copy-done((f32[128,512]{1,0:T(8,128)S(1)}, f32[128,512]{1,0:T(8,128)}, u32[]{:S(2)}) %copy-start.2) | copy-done | bytes 262168
  55.7 1.3 %shard_map.102 = (f32[128,256]{1,0:T(8,128)}, f32[256,256]{1,0:T(8,128)}, f32[256,256]{1,0:T(8,128)}, f32[128,256]{1,0:T(8,128)}, f32[256,256]{1,0:T(8,128)}) custom-call(f32[128,512]{1,0:T(8,128)S(1)} %copy-done.2, f32[1536,128]{1,0:T(8,128)S(1)} %copy-done, bf16[256,256]{1,0:T(8,128)(2,1)S(1)} %copy-done.3, f32[2,256,256]{2,1,0:T(8,128)S(1)} %copy-done.1), custom_call_target="tpu_custom_call" | custom-call | tf_op jit(solution)/shard_map/pallas_call | solution.py:403
Async XLA Ops:
  2.0 51.6 %copy-start.1 = (f32[2,256,256]{2,1,0:T(8,128)S(1)}, f32[2,256,256]{2,1,0:T(8,128)}, u32[]{:S(2)}) copy-start(f32[2,256,256]{2,1,0:T(8,128)} %piv_ref.1) | copy-start | bytes 1572868
  2.0 51.6 %copy-start.3 = (bf16[256,256]{1,0:T(8,128)(2,1)S(1)}, bf16[256,256]{1,0:T(8,128)(2,1)}, u32[]{:S(2)}) copy-start(bf16[256,256]{1,0:T(8,128)(2,1)} %top_ref.1) | copy-start | bytes 393220
  53.6 1.1 %copy-start = (f32[1536,128]{1,0:T(8,128)S(1)}, f32[1536,128]{1,0:T(8,128)}, u32[]{:S(2)}) copy-start(f32[1536,128]{1,0:T(8,128)} %get-tuple-element.8.g_ref) | copy-start | bytes 2359300
  54.7 0.9 %copy-start.2 = (f32[128,512]{1,0:T(8,128)S(1)}, f32[128,512]{1,0:T(8,128)}, u32[]{:S(2)}) copy-start(f32[128,512]{1,0:T(8,128)} %get-tuple-element.7.sum_ref) | copy-start | bytes 786436

commit v3 on v2

--- a/solution.py
+++ b/solution.py
@@ -159,7 +159,7 @@
     for b in range(rows // BLOCK):
         for j in range(cols // BLOCK):
             tile = (slice(b * BLOCK, (b + 1) * BLOCK), slice(j * BLOCK, (j + 1) * BLOCK))
-            keep = tm_ref[b : b + 1, j : j + 1].astype(F32)
+            keep = tm_ref[j : j + 1, b : b + 1].astype(F32)
             mk[tile] = (m_ref[tile].astype(F32) * keep).astype(BF16)
     for e in range(nr):
         g = lax.rem(z + 1 + e, nr)
@@ -207,6 +207,29 @@
         to = lax.rem(r + d, nr)
         start(gps.at[to], grs.at[d - 1], as_sem.at[1, d - 1], ar_sem.at[1, d - 1], to, c)
         start(at(gpq, to * grows, grows), grq.at[d - 1], as_sem.at[0, d - 1], ar_sem.at[0, d - 1], to, c)
+    for e in range(1, ratio):
+        panels_arrive(e)
+    zlines = kr // GROUP
+
+    def send_rows(e):
+        to = lax.rem(z + 1 + e, nr) * ratio + x
+        start(zx.at[e], zrx.at[e], zs_sem.at[1, e], zr_sem.at[1, e], r, to)
+        start(zq.at[e], zrq.at[e], zs_sem.at[0, e], zr_sem.at[0, e], r, to)
+
+    for e in range(nr):
+        g = lax.rem(z + 1 + e, nr)
+        value = q[pl.ds(pl.multiple_of((g * ratio + x) * kr, 16), kr), :]
+        for d in range(1, ratio):
+            arrived(mx.at[d - 1, e], ms_sem.at[d - 1, e], mr_sem.at[d - 1, e])
+            half = lax.rem(x - d + ratio, ratio)
+            value = value + dot(mx[d - 1, e], jz[pl.ds(pl.multiple_of(half * cols, cols), cols), :])
+        if e < nr - 1:
+            zq[e], zx[e, :zlines, :] = quantize(value)
+            if e == 0:
+                send_rows(e)
+        else:
+            own[...] = value
+
     total = gp[pl.ds(pl.multiple_of(r * grows, 16), grows), :]
     for d in range(1, nr):
         arrived(grs.at[d - 1], as_sem.at[1, d - 1], ar_sem.at[1, d - 1])
@@ -226,23 +249,8 @@
     gcs[pl.ds(c, 1)] = gts[pl.ds(place, 1)]
     gcq[pl.ds(c, 1)] = gtq[pl.ds(pl.multiple_of(place * gcols, 16), gcols), :][None]
 
-    for e in range(1, ratio):
-        panels_arrive(e)
-    zlines = kr // GROUP
-    for e in range(nr):
-        g = lax.rem(z + 1 + e, nr)
-        value = q[pl.ds(pl.multiple_of((g * ratio + x) * kr, 16), kr), :]
-        for d in range(1, ratio):
-            arrived(mx.at[d - 1, e], ms_sem.at[d - 1, e], mr_sem.at[d - 1, e])
-            half = lax.rem(x - d + ratio, ratio)
-            value = value + dot(mx[d - 1, e], jz[pl.ds(pl.multiple_of(half * cols, cols), cols), :])
-        if e < nr - 1:
-            zq[e], zx[e, :zlines, :] = quantize(value)
-            to = g * ratio + x
-            start(zx.at[e], zrx.at[e], zs_sem.at[1, e], zr_sem.at[1, e], r, to)
-            start(zq.at[e], zrq.at[e], zs_sem.at[0, e], zr_sem.at[0, e], r, to)
-        else:
-            own[...] = value
+    for e in range(1, nr - 1):
+        send_rows(e)
 
     total = None
     for d in range(1, nc):
@@ -357,12 +365,12 @@
     I16 = jnp.int16
     summed, small_sums = pl.pallas_call(
         functools.partial(kernel, nr, nc),
-        out_shape=(jax.ShapeDtypeStruct((kr, 2 * width), F32), jax.ShapeDtypeStruct((small, BLOCK), F32)),
+        out_shape=(pltpu.VMEM((kr, 2 * width), F32), pltpu.VMEM((small, BLOCK), F32)),
         in_specs=[anywhere] * 4,
         out_specs=(vmem,) * 2,
         scratch_shapes=[
             pltpu.VMEM(inverse_block.shape, BF16),
-            pltpu.VMEM(tile_mask.shape, jnp.int32),
+            pltpu.VMEM(tile_mask.shape[::-1], jnp.int32),
             pltpu.VMEM(factor.shape, BF16),
             pltpu.VMEM(panel_mask.shape, jnp.int32),
             pltpu.VMEM((rows, cols), BF16),
@@ -399,7 +407,7 @@
         compiler_params=pltpu.CompilerParams(
             collective_id=0, has_side_effects=True, vmem_limit_bytes=56 * 1024 * 1024
         ),
-    )(inverse_block, tile_mask, factor, panel_mask)
+    )(inverse_block, tile_mask.T, factor, panel_mask)
     return pl.pallas_call(
         finish,
         out_shape=(column, square, square, column, square),

time: 57.9 us -> 50.5 us (0.87); the launches traced: 56.9 us -> 50.4 us
  local copies, waits for them, and re-layouts: 3.43 us -> 0.01 us
  Pallas kernels: 52.8 us -> 49.7 us
    unnamed x9 -> x4, local copies, waits for them, and re-layouts: 3.43 us -> 0.01 us
    pallas_call x1, Pallas kernels: 51.6 us -> 48.4 us  [shards(): pl.pallas_call(functools.partial(kernel, nr, nc), out_shape=(pltpu.VMEM((...]
where the time goes in v3:
time: 50.5 us; the launch traced here: 50.4 us
  Pallas kernels  49.7 us (98%)
  between operations  0.67 us (1%)
    pallas_call x1, Pallas kernels, shards(): pl.pallas_call(functools.partial(kernel, nr, nc), out_shape=(pltpu.VMEM((...  48.4 us
    pallas_call x1, Pallas kernels, shards(): pl.pallas_call(finish, out_shape=(column, square, square, column, square)...  1.27 us

profile of v3, /device:TPU:0, one launch (start us, length us, event | category | flops | bytes accessed | tf_op | source)
XLA Modules:
  0.0 50.4 jit_solution(11105834997392874388)
XLA Ops:
  0.6 0.0 copy-start
  0.6 0.0 copy-start.1
  0.7 48.4 %shard_map.101 = (f32[128,512]{1,0:T(8,128)S(1)}, f32[1536,128]{1,0:T(8,128)S(1)}) custom-call(bf16[1024,512]{1,0:T(8,128)(2,1)} %m_any.1, s32[4,8]{1,0:T(4,128)} %bitcast.1, bf16[2,1024,256]{2,1,0:T(8,128)(2,1)} %f_any.1, s32[2,8]{1,0:T(2,128)} %pm_any.1), custom_call_target="tpu_custom_call" | custom-call | tf_op jit(solution)/shard_map/pallas_call | solution.py:366
  49.1 0.0 copy-done
  49.1 0.0 copy-done.1
  49.1 1.3 %shard_map.102 = (f32[128,256]{1,0:T(8,128)}, f32[256,256]{1,0:T(8,128)}, f32[256,256]{1,0:T(8,128)}, f32[128,256]{1,0:T(8,128)}, f32[256,256]{1,0:T(8,128)}) custom-call(f32[128,512]{1,0:T(8,128)S(1)} %get-tuple-element.7.sum_ref, f32[1536,128]{1,0:T(8,128)S(1)} %get-tuple-element.8.g_ref, bf16[256,256]{1,0:T(8,128)(2,1)S(1)} %copy-done.1, ...), custom_call_target="tpu_custom_call" | custom-call | tf_op jit(solution)/shard_map/pallas_call | solution.py:411
Async XLA Ops:
  0.6 48.4 %copy-start = (f32[2,256,256]{2,1,0:T(8,128)S(1)}, f32[2,256,256]{2,1,0:T(8,128)}, u32[]{:S(2)}) copy-start(f32[2,256,256]{2,1,0:T(8,128)} %piv_ref.1) | copy-start | bytes 1572868
  0.6 48.4 %copy-start.1 = (bf16[256,256]{1,0:T(8,128)(2,1)S(1)}, bf16[256,256]{1,0:T(8,128)(2,1)}, u32[]{:S(2)}) copy-start(bf16[256,256]{1,0:T(8,128)(2,1)} %top_ref.1) | copy-start | bytes 393220

commit v4 on v2

v4 whole, which is shorter than its diff:
```python
import functools

import jax
import jax.numpy as jnp
from jax import lax
from jax.experimental import pallas as pl
from jax.experimental.pallas import tpu as pltpu
from jax.sharding import PartitionSpec as P

BLOCK = 128
GROUP = 16
MESH = pl.DeviceIdType.MESH
F32 = jnp.float32
BF16 = jnp.bfloat16


def split(a):
    high = a.astype(BF16)
    return high, (a - high.astype(F32)).astype(BF16)


def dot(a, b):
    return jnp.dot(a, b, preferred_element_type=F32)


def dot_t(a, b):
    return lax.dot_general(a, b, (((0,), (0,)), ((), ())), preferred_element_type=F32)


def packed(rows):
    return rows + -(-(rows // GROUP) // GROUP) * GROUP


def pack(a):
    groups = a.shape[0] // GROUP
    parts = a.reshape(groups, GROUP, a.shape[1])
    largest = jnp.maximum(jnp.max(jnp.abs(parts), axis=1), 1e-30)
    power = jnp.ceil(jnp.log2(largest) - 14.99)
    whole = jnp.round(parts * jnp.exp2(-power)[:, None, :]).astype(jnp.int32)
    whole = whole.reshape(a.shape).astype(jnp.int16)
    padding = packed(a.shape[0]) - a.shape[0] - groups
    if padding:
        power = jnp.concatenate([power, jnp.zeros((padding, a.shape[1]), F32)], axis=0)
    return jnp.concatenate([whole, power.astype(jnp.int32).astype(jnp.int16)], axis=0)


def unpack(held, rows):
    groups = rows // GROUP
    scale = jnp.exp2(held[rows:].astype(jnp.int32).astype(F32))[:groups]
    parts = held[:rows].astype(jnp.int32).astype(F32).reshape(groups, GROUP, held.shape[1])
    return (parts * scale[:, None, :]).reshape(rows, held.shape[1])


def kernel(
    nr, nc, lots, m_any, tm_any, f_any, pm_any, sum_ref, g_ref,
    m_ref, tm_ref, f_ref, pm_ref, mk, jown, jt, jz, mx, q, zq, zrq,
    hf, h1, h1r, h2, h2r, gt, gc, gf, in_sem,
    ps_sem, pr_sem, fs_sem, ms_sem, mr_sem, zs_sem, zr_sem,
    as_sem, ar_sem, es_sem, er_sem, bs_sem, br_sem, cs_sem, cr_sem, ds_sem, dr_sem, xs_sem, xr_sem,
):
    r, c = lax.axis_index("row"), lax.axis_index("col")
    ratio = nc // nr
    rows, cols = m_ref.shape
    width = f_ref.shape[2]
    kr = rows // nc
    qr = cols // 2
    grows = g_ref.shape[0] // nr
    shared = lots == 1
    gcols = grows // lots
    share = width // nr
    hrows = 2 * share
    x, z = lax.rem(c, ratio), lax.div(c, ratio)
    chip, core = lax.div(r, 2), lax.rem(r, 2)
    chips = nr // 2
    mate = chip * 2 + 1 - core
    is_source = r == z
    same_chip = chip == lax.div(z, 2)
    sent = []

    loads = [
        pltpu.make_async_copy(there, here, in_sem.at[i])
        for i, (there, here) in enumerate(
            ((pm_any, pm_ref), (f_any, f_ref), (tm_any, tm_ref), (m_any, m_ref))
        )
    ]
    for load in loads:
        load.start()

    def copy(src, dst, send, recv, row, col):
        return pltpu.make_async_remote_copy(
            src_ref=src, dst_ref=dst, send_sem=send, recv_sem=recv,
            device_id=(row, col), device_id_type=MESH,
        )

    def start(src, dst, send, recv, row, col):
        made = copy(src, dst, send, recv, row, col)
        made.start()
        sent.append(made)

    def arrived(dst, send, recv):
        copy(dst, dst, send, recv, r, c).wait_recv()

    def at(ref, first, count):
        return ref.at[pl.ds(pl.multiple_of(first, 16), count)]

    barrier = pltpu.get_barrier_semaphore()
    for d in range(1, nr):
        pl.semaphore_signal(
            barrier, inc=1, device_id=(lax.rem(r + d, nr), c), device_id_type=MESH
        )
    for d in range(1, nc):
        pl.semaphore_signal(
            barrier, inc=1, device_id=(r, lax.rem(c + d, nc)), device_id_type=MESH
        )
    loads[0].wait()
    loads[1].wait()
    for b in range(rows // BLOCK):
        part = slice(b * BLOCK, (b + 1) * BLOCK)
        for s in range(2):
            keep = pm_ref[s : s + 1, b : b + 1].astype(F32)
            jown[part, s * width : (s + 1) * width] = (f_ref[s, part, :].astype(F32) * keep).astype(BF16)
    pl.semaphore_wait(barrier, nr + nc - 2)

    def piece(ref, e, h):
        half = lax.rem(x + e, ratio)
        return at(ref, (half * 2 + h) * qr, qr)

    def panel_copies(e):
        made = []
        for h in range(2):
            i = 2 * e + h
            for d in range(1, chips):
                to = lax.rem(chip + d, chips) * 2 + h
                made.append(
                    copy(piece(jown, e, h), piece(jz, e, h), ps_sem.at[i, d], pr_sem.at[i], to, c)
                )
            made.append(
                copy(piece(jown, e, h), piece(jz, e, h), ps_sem.at[i, 0], pr_sem.at[i], mate, c)
            )
        return made

    def forward_copy(e):
        half = lax.rem(x + e, ratio)
        part = at(jz, (half * 2 + core) * qr, qr)
        i = 2 * e + core
        return part, copy(part, part, fs_sem.at[e], pr_sem.at[i], mate, c)

    def panels_arrive(e):
        @pl.when(jnp.logical_and(jnp.logical_not(is_source), same_chip))
        def _():
            for h in range(2):
                arrived(piece(jz, e, h), ps_sem.at[2 * e + h, 0], pr_sem.at[2 * e + h])

        @pl.when(jnp.logical_not(same_chip))
        def _():
            part, made = forward_copy(e)
            arrived(part, fs_sem.at[e], pr_sem.at[2 * e + core])
            made.start()
            half = lax.rem(x + e, ratio)
            other = at(jz, (half * 2 + 1 - core) * qr, qr)
            arrived(other, fs_sem.at[e], pr_sem.at[2 * e + 1 - core])

    @pl.when(is_source)
    def _():
        for made in panel_copies(0):
            made.start()

    loads[2].wait()
    loads[3].wait()
    for b in range(rows // BLOCK):
        for j in range(cols // BLOCK):
            tile = (slice(b * BLOCK, (b + 1) * BLOCK), slice(j * BLOCK, (j + 1) * BLOCK))
            keep = tm_ref[j : j + 1, b : b + 1].astype(F32)
            mk[tile] = (m_ref[tile].astype(F32) * keep).astype(BF16)
    for e in range(nr):
        g = lax.rem(z + 1 + e, nr)
        for d in range(1, ratio):
            xx = lax.rem(x + d, ratio)
            start(
                at(mk, (g * ratio + xx) * kr, kr), mx.at[d - 1, e],
                ms_sem.at[d - 1, e], mr_sem.at[d - 1, e], r, z * ratio + xx,
            )

    jt[...] = jown[...].T
    for i in range(2):
        for k in range(2 * width // 256):
            part = slice(k * 256, (k + 1) * 256)
            half = slice(i * cols // 2, (i + 1) * cols // 2)
            hf[part, half] = dot(jt[part, :], mk[:, half])

    def chunk(to):
        first = pl.multiple_of(to * share, 16)
        return jnp.concatenate([hf[pl.ds(first, share), :], hf[pl.ds(width + first, share), :]], axis=0)

    for i in range(chips):
        h1[i] = pack(chunk(i * 2 + 1 - core))
    start(h1, h1r, as_sem.at[0], ar_sem.at[0], mate, c)
    arrived(h1r, as_sem.at[0], ar_sem.at[0])
    for d in range(1, chips):
        there = lax.rem(chip + d, chips)
        h2[d - 1] = pack(chunk(there * 2 + core) + unpack(h1r[there], hrows))
        start(h2.at[d - 1], h2r.at[d - 1], es_sem.at[d - 1], er_sem.at[d - 1], there * 2 + core, c)

    @pl.when(is_source)
    def _():
        jz[...] = jown[...]
        for made in panel_copies(0):
            made.wait_send()
        for e in range(1, ratio):
            for made in panel_copies(e):
                made.start()

    total = chunk(r) + unpack(h1r[chip], hrows)

    panels_arrive(0)
    near = jz[pl.ds(pl.multiple_of(x * cols, cols), cols), :]
    for e in range(nr):
        g = lax.rem(z + 1 + e, nr)
        q[e] = dot(mk[pl.ds(pl.multiple_of((g * ratio + x) * kr, 16), kr), :], near)

    for d in range(1, chips):
        arrived(h2r.at[d - 1], es_sem.at[d - 1], er_sem.at[d - 1])
        total = total + unpack(h2r[d - 1], hrows)
    high, low = split(total)
    parent = dot(high[:share], near[:, :width]) + dot(low[:share], near[:, :width])
    both = dot(high[share:], near) + dot(low[share:], near)
    slots = width // BLOCK
    pieces = [parent[:, j * BLOCK : (j + 1) * BLOCK] for j in range(slots)]
    pieces += [both[:, j * BLOCK : (j + 1) * BLOCK] for j in range(2 * slots)]
    total = jnp.concatenate(pieces, axis=0)

    for i in range(lots):
        gt[i] = pack(total[i * gcols : (i + 1) * gcols, :])
    for d in range(1, nc):
        to = lax.rem(c + d, nc)
        start(gt.at[0 if shared else to], gc.at[c], bs_sem.at[d - 1], br_sem.at[d - 1], r, to)
    place = 0 if shared else c
    gc[pl.ds(c, 1)] = gt[pl.ds(place, 1)]

    for e in range(1, ratio):
        panels_arrive(e)
    for e in range(nr):
        value = q[e]
        for d in range(1, ratio):
            arrived(mx.at[d - 1, e], ms_sem.at[d - 1, e], mr_sem.at[d - 1, e])
            half = lax.rem(x - d + ratio, ratio)
            value = value + dot(mx[d - 1, e], jz[pl.ds(pl.multiple_of(half * cols, cols), cols), :])
        if e < nr - 1:
            zq[e] = pack(value)
            to = lax.rem(z + 1 + e, nr) * ratio + x
            start(zq.at[e], zrq.at[e], zs_sem.at[e], zr_sem.at[e], r, to)
        else:
            q[e] = value

    for d in range(1, nc):
        come = lax.rem(c + nc - d, nc)
        arrived(gc.at[come], bs_sem.at[d - 1], br_sem.at[d - 1])
    total = unpack(gc[0], gcols)
    for i in range(1, nc):
        total = total + unpack(gc[i], gcols)
    gf[r, place] = pack(total)
    if not shared:
        for d in range(1, nc):
            to = lax.rem(c + d, nc)
            start(gf.at[r, c], gf.at[r, c], cs_sem.at[d - 1], cr_sem.at[d - 1], r, to)
        for d in range(1, nc):
            come = lax.rem(c + nc - d, nc)
            arrived(gf.at[r, come], cs_sem.at[d - 1], cr_sem.at[d - 1])
    for d in range(1, chips):
        to = lax.rem(chip + d, chips) * 2 + core
        start(gf.at[r], gf.at[r], ds_sem.at[d - 1], dr_sem.at[d - 1], to, c)
    start(gf.at[r], gf.at[r], xs_sem.at[0], xr_sem.at[0], mate, c)
    for d in range(1, chips):
        come = lax.rem(chip + chips - d, chips) * 2 + core
        arrived(gf.at[come], ds_sem.at[d - 1], dr_sem.at[d - 1])
        start(gf.at[come], gf.at[come], xs_sem.at[d], xr_sem.at[d], mate, c)

    value = q[nr - 1]
    for e in range(nr - 1):
        arrived(zrq.at[e], zs_sem.at[e], zr_sem.at[e])
        value = value + unpack(zrq[e], kr)
    sum_ref[...] = value

    for d in range(chips):
        come = lax.rem(chip + chips - d, chips) * 2 + 1 - core
        arrived(gf.at[come], xs_sem.at[d], xr_sem.at[d])
    for i in range(nr):
        block = jnp.concatenate([unpack(gf[i, j], gcols) for j in range(lots)], axis=0)
        for k in range(3 * slots):
            g_ref[k * width + i * share : k * width + (i + 1) * share, :] = block[k * share : (k + 1) * share, :]

    for made in sent:
        made.wait_send()

    @pl.when(is_source)
    def _():
        for e in range(1, ratio):
            for made in panel_copies(e):
                made.wait_send()

    @pl.when(jnp.logical_not(same_chip))
    def _():
        for e in range(ratio):
            forward_copy(e)[1].wait_send()


def finish(sum_ref, g_ref, top_ref, piv_ref, pc_ref, pd_ref, cu_ref, cc_ref, cd_ref):
    width = top_ref.shape[0]
    slots = width // BLOCK
    top = top_ref[...]
    value = sum_ref[...]
    parent = value[:, :width]
    high, low = split(parent)
    pc_ref[...] = -parent
    cc_ref[...] = dot(high, top) + dot(low, top) - value[:, width:]

    def square(i):
        return jnp.concatenate(
            [g_ref[(i * slots + j) * width : (i * slots + j + 1) * width, :] for j in range(slots)], axis=1
        )

    diag = piv_ref[0] + square(0)
    pd_ref[...] = diag
    cross = square(1)
    high, low = split(diag)
    upper = cross.T - (dot(high, top) + dot(low, top))
    cu_ref[...] = upper
    high, low = split(upper)
    cross_high, cross_low = split(cross)
    cd_ref[...] = (
        piv_ref[1] - (dot_t(top, high) + dot_t(top, low))
        - (dot(cross_high, top) + dot(cross_low, top)) + square(2)
    )


def shards(nr, nc, inverse_block, tile_mask, factor, panel_mask, child_top, pivots):
    rows, cols = inverse_block.shape
    width = factor.shape[2]
    ratio = nc // nr
    kr = rows // nc
    small = 3 * width * width // BLOCK
    grows = small // nr
    lots = nc if grows % (GROUP * nc) == 0 else 1
    gcols = grows // lots
    dma = pltpu.SemaphoreType.DMA
    vmem, anywhere = pl.BlockSpec(memory_space=pltpu.VMEM), pl.BlockSpec(memory_space=pl.ANY)
    square = jax.ShapeDtypeStruct((width, width), F32)
    column = jax.ShapeDtypeStruct((kr, width), F32)
    others = max(ratio - 1, 1)
    chips, hrows = nr // 2, 2 * width // nr
    I16 = jnp.int16
    summed, small_sums = pl.pallas_call(
        functools.partial(kernel, nr, nc, lots),
        out_shape=(pltpu.VMEM((kr, 2 * width), F32), pltpu.VMEM((small, BLOCK), F32)),
        in_specs=[anywhere] * 4,
        out_specs=(vmem,) * 2,
        scratch_shapes=[
            pltpu.VMEM(inverse_block.shape, BF16),
            pltpu.VMEM(tile_mask.shape[::-1], jnp.int32),
            pltpu.VMEM(factor.shape, BF16),
            pltpu.VMEM(panel_mask.shape, jnp.int32),
            pltpu.VMEM((rows, cols), BF16),
            pltpu.VMEM((rows, 2 * width), BF16),
            pltpu.VMEM((2 * width, rows), BF16),
            pltpu.VMEM((rows, 2 * width), BF16),
            pltpu.VMEM((others, nr, kr, cols), BF16),
            pltpu.VMEM((nr, kr, 2 * width), F32),
            pltpu.VMEM((nr - 1, packed(kr), 2 * width), I16),
            pltpu.VMEM((nr - 1, packed(kr), 2 * width), I16),
            pltpu.VMEM((2 * width, cols), F32),
            pltpu.VMEM((chips, packed(hrows), cols), I16),
            pltpu.VMEM((chips, packed(hrows), cols), I16),
            pltpu.VMEM((chips - 1, packed(hrows), cols), I16),
            pltpu.VMEM((chips - 1, packed(hrows), cols), I16),
            pltpu.VMEM((lots, packed(gcols), BLOCK), I16),
            pltpu.VMEM((nc, packed(gcols), BLOCK), I16),
            pltpu.VMEM((nr, lots, packed(gcols), BLOCK), I16),
            dma((4,)),
            dma((2 * ratio, max(nr // 2, 1))), dma((2 * ratio,)), dma((ratio,)),
            dma((others, nr)), dma((others, nr)),
            dma((nr - 1,)), dma((nr - 1,)),
            dma((1,)), dma((1,)), dma((chips - 1,)), dma((chips - 1,)),
            dma((nc - 1,)), dma((nc - 1,)), dma((nc - 1,)), dma((nc - 1,)),
            dma((chips - 1,)), dma((chips - 1,)), dma((chips,)), dma((chips,)),
        ],
        compiler_params=pltpu.CompilerParams(
            collective_id=0, has_side_effects=True, vmem_limit_bytes=56 * 1024 * 1024
        ),
    )(inverse_block, tile_mask.T, factor, panel_mask)
    return pl.pallas_call(
        finish,
        out_shape=(column, square, square, column, square),
        in_specs=[vmem] * 4,
        out_specs=(vmem,) * 5,
        compiler_params=pltpu.CompilerParams(vmem_limit_bytes=24 * 1024 * 1024),
    )(summed, small_sums, child_top, pivots)


def solution(mesh):
    in_specs = (P("row", "col"), P("row", "col"), P(None, "row", None), P(None, "row"), P(), P())
    out_specs = (P(("row", "col"), None), P(), P(), P(("row", "col"), None), P())
    body = functools.partial(shards, mesh.shape["row"], mesh.shape["col"])
    return jax.shard_map(body, mesh=mesh, in_specs=in_specs, out_specs=out_specs, check_vma=False)
```

time: 57.9 us -> 46.7 us (0.81)
  the two profiles are of different devices: /device:TPU:0 before, /device:TPU:5 now
where the time goes in v4:
time: 46.7 us; the launch traced here: 46.5 us
  Pallas kernels  45.9 us (98%)
  between operations  0.67 us (1%)
    pallas_call x1, Pallas kernels, shards(): pl.pallas_call(functools.partial(kernel, nr, nc, lots), out_shape=(pltpu....  44.6 us
    pallas_call x1, Pallas kernels, shards(): pl.pallas_call(finish, out_shape=(column, square, square, column, square)...  1.27 us

profile of v4, /device:TPU:5, one launch (start us, length us, event | category | flops | bytes accessed | tf_op | source)
XLA Modules:
  0.0 46.5 jit_solution(154872185625537457)
XLA Ops:
  0.6 0.0 copy-start
  0.6 0.0 copy-start.1
  0.7 44.6 %shard_map.101 = (f32[128,512]{1,0:T(8,128)S(1)}, f32[1536,128]{1,0:T(8,128)S(1)}) custom-call(bf16[1024,512]{1,0:T(8,128)(2,1)} %m_any.1, s32[4,8]{1,0:T(4,128)} %bitcast.1, bf16[2,1024,256]{2,1,0:T(8,128)(2,1)} %f_any.1, s32[2,8]{1,0:T(2,128)} %pm_any.1), custom_call_target="tpu_custom_call" | custom-call | tf_op jit(solution)/shard_map/pallas_call | solution.py:352
  45.2 0.0 copy-done
  45.3 0.0 copy-done.1
  45.3 1.3 %shard_map.102 = (f32[128,256]{1,0:T(8,128)}, f32[256,256]{1,0:T(8,128)}, f32[256,256]{1,0:T(8,128)}, f32[128,256]{1,0:T(8,128)}, f32[256,256]{1,0:T(8,128)}) custom-call(f32[128,512]{1,0:T(8,128)S(1)} %get-tuple-element.7.sum_ref, f32[1536,128]{1,0:T(8,128)S(1)} %get-tuple-element.8.g_ref, bf16[256,256]{1,0:T(8,128)(2,1)S(1)} %copy-done.1, ...), custom_call_target="tpu_custom_call" | custom-call | tf_op jit(solution)/shard_map/pallas_call | solution.py:390
Async XLA Ops:
  0.6 44.6 %copy-start = (f32[2,256,256]{2,1,0:T(8,128)S(1)}, f32[2,256,256]{2,1,0:T(8,128)}, u32[]{:S(2)}) copy-start(f32[2,256,256]{2,1,0:T(8,128)} %piv_ref.1) | copy-start | bytes 1572868
  0.6 44.6 %copy-start.1 = (bf16[256,256]{1,0:T(8,128)(2,1)S(1)}, bf16[256,256]{1,0:T(8,128)(2,1)}, u32[]{:S(2)}) copy-start(bf16[256,256]{1,0:T(8,128)(2,1)} %top_ref.1) | copy-start | bytes 393220

commit v5 on v4

--- a/solution.py
+++ b/solution.py
@@ -9,6 +9,7 @@
 
 BLOCK = 128
 GROUP = 16
+WIDE = 32
 MESH = pl.DeviceIdType.MESH
 F32 = jnp.float32
 BF16 = jnp.bfloat16
@@ -27,28 +28,36 @@
     return lax.dot_general(a, b, (((0,), (0,)), ((), ())), preferred_element_type=F32)
 
 
-def packed(rows):
-    return rows + -(-(rows // GROUP) // GROUP) * GROUP
-
-
-def pack(a):
-    groups = a.shape[0] // GROUP
-    parts = a.reshape(groups, GROUP, a.shape[1])
+def packed(rows, group=GROUP):
+    return rows + -(-(rows // group) // 16) * 16
+
+
+def pack(a, group=GROUP):
+    groups = a.shape[0] // group
+    parts = a.reshape(groups, group, a.shape[1])
     largest = jnp.maximum(jnp.max(jnp.abs(parts), axis=1), 1e-30)
     power = jnp.ceil(jnp.log2(largest) - 14.99)
     whole = jnp.round(parts * jnp.exp2(-power)[:, None, :]).astype(jnp.int32)
     whole = whole.reshape(a.shape).astype(jnp.int16)
-    padding = packed(a.shape[0]) - a.shape[0] - groups
+    padding = packed(a.shape[0], group) - a.shape[0] - groups
     if padding:
         power = jnp.concatenate([power, jnp.zeros((padding, a.shape[1]), F32)], axis=0)
     return jnp.concatenate([whole, power.astype(jnp.int32).astype(jnp.int16)], axis=0)
 
 
-def unpack(held, rows):
-    groups = rows // GROUP
+def unpack(held, rows, group=GROUP):
+    groups = rows // group
     scale = jnp.exp2(held[rows:].astype(jnp.int32).astype(F32))[:groups]
-    parts = held[:rows].astype(jnp.int32).astype(F32).reshape(groups, GROUP, held.shape[1])
+    parts = held[:rows].astype(jnp.int32).astype(F32).reshape(groups, group, held.shape[1])
     return (parts * scale[:, None, :]).reshape(rows, held.shape[1])
+
+
+def fold(a):
+    return jnp.concatenate([a[:, j : j + BLOCK] for j in range(0, a.shape[1], BLOCK)], axis=0)
+
+
+def unfold(a, rows):
+    return jnp.concatenate([a[i : i + rows] for i in range(0, a.shape[0], rows)], axis=1)
 
 
 def kernel(
@@ -61,6 +70,7 @@
     r, c = lax.axis_index("row"), lax.axis_index("col")
     ratio = nc // nr
     rows, cols = m_ref.shape
+    x, z = lax.rem(c, ratio), lax.div(c, ratio)
     width = f_ref.shape[2]
     kr = rows // nc
     qr = cols // 2
@@ -69,7 +79,17 @@
     gcols = grows // lots
     share = width // nr
     hrows = 2 * share
-    x, z = lax.rem(c, ratio), lax.div(c, ratio)
+    hlong = hrows * cols // BLOCK
+    zlong = kr * 2 * width // BLOCK
+    half = nr // 2
+    pair, side = lax.div(z, 2), lax.rem(z, 2)
+
+    def pair_dest(m, which):
+        return lax.rem(pair + m, half) * 2 + which
+
+    order = [pair_dest(m, 1 - side) for m in range(1, half)]
+    order += [pair_dest(m, side) for m in range(1, half)]
+    order += [pair_dest(0, 1 - side), z]
     chip, core = lax.div(r, 2), lax.rem(r, 2)
     chips = nr // 2
     mate = chip * 2 + 1 - core
@@ -122,8 +142,8 @@
     pl.semaphore_wait(barrier, nr + nc - 2)
 
     def piece(ref, e, h):
-        half = lax.rem(x + e, ratio)
-        return at(ref, (half * 2 + h) * qr, qr)
+        part_of = lax.rem(x + e, ratio)
+        return at(ref, (part_of * 2 + h) * qr, qr)
 
     def panel_copies(e):
         made = []
@@ -140,10 +160,17 @@
         return made
 
     def forward_copy(e):
-        half = lax.rem(x + e, ratio)
-        part = at(jz, (half * 2 + core) * qr, qr)
+        part_of = lax.rem(x + e, ratio)
+        part = at(jz, (part_of * 2 + core) * qr, qr)
         i = 2 * e + core
         return part, copy(part, part, fs_sem.at[e], pr_sem.at[i], mate, c)
+
+    def panels_forward(e):
+        @pl.when(jnp.logical_not(same_chip))
+        def _():
+            part, made = forward_copy(e)
+            arrived(part, fs_sem.at[e], pr_sem.at[2 * e + core])
+            made.start()
 
     def panels_arrive(e):
         @pl.when(jnp.logical_and(jnp.logical_not(is_source), same_chip))
@@ -153,11 +180,7 @@
 
         @pl.when(jnp.logical_not(same_chip))
         def _():
-            part, made = forward_copy(e)
-            arrived(part, fs_sem.at[e], pr_sem.at[2 * e + core])
-            made.start()
-            half = lax.rem(x + e, ratio)
-            other = at(jz, (half * 2 + 1 - core) * qr, qr)
+            other = at(jz, (lax.rem(x + e, ratio) * 2 + 1 - core) * qr, qr)
             arrived(other, fs_sem.at[e], pr_sem.at[2 * e + 1 - core])
 
     @pl.when(is_source)
@@ -172,8 +195,7 @@
             tile = (slice(b * BLOCK, (b + 1) * BLOCK), slice(j * BLOCK, (j + 1) * BLOCK))
             keep = tm_ref[j : j + 1, b : b + 1].astype(F32)
             mk[tile] = (m_ref[tile].astype(F32) * keep).astype(BF16)
-    for e in range(nr):
-        g = lax.rem(z + 1 + e, nr)
+    for e, g in enumerate(order):
         for d in range(1, ratio):
             xx = lax.rem(x + d, ratio)
             start(
@@ -185,20 +207,20 @@
     for i in range(2):
         for k in range(2 * width // 256):
             part = slice(k * 256, (k + 1) * 256)
-            half = slice(i * cols // 2, (i + 1) * cols // 2)
-            hf[part, half] = dot(jt[part, :], mk[:, half])
+            span = slice(i * cols // 2, (i + 1) * cols // 2)
+            hf[part, span] = dot(jt[part, :], mk[:, span])
 
     def chunk(to):
         first = pl.multiple_of(to * share, 16)
-        return jnp.concatenate([hf[pl.ds(first, share), :], hf[pl.ds(width + first, share), :]], axis=0)
+        return fold(jnp.concatenate([hf[pl.ds(first, share), :], hf[pl.ds(width + first, share), :]], axis=0))
 
     for i in range(chips):
-        h1[i] = pack(chunk(i * 2 + 1 - core))
+        h1[i] = pack(chunk(i * 2 + 1 - core), WIDE)
     start(h1, h1r, as_sem.at[0], ar_sem.at[0], mate, c)
     arrived(h1r, as_sem.at[0], ar_sem.at[0])
     for d in range(1, chips):
         there = lax.rem(chip + d, chips)
-        h2[d - 1] = pack(chunk(there * 2 + core) + unpack(h1r[there], hrows))
+        h2[d - 1] = pack(chunk(there * 2 + core) + unpack(h1r[there], hlong, WIDE), WIDE)
         start(h2.at[d - 1], h2r.at[d - 1], es_sem.at[d - 1], er_sem.at[d - 1], there * 2 + core, c)
 
     @pl.when(is_source)
@@ -210,17 +232,18 @@
             for made in panel_copies(e):
                 made.start()
 
-    total = chunk(r) + unpack(h1r[chip], hrows)
-
+    total = chunk(r) + unpack(h1r[chip], hlong, WIDE)
+
+    panels_forward(0)
     panels_arrive(0)
     near = jz[pl.ds(pl.multiple_of(x * cols, cols), cols), :]
-    for e in range(nr):
-        g = lax.rem(z + 1 + e, nr)
+    for e, g in enumerate(order):
         q[e] = dot(mk[pl.ds(pl.multiple_of((g * ratio + x) * kr, 16), kr), :], near)
 
     for d in range(1, chips):
         arrived(h2r.at[d - 1], es_sem.at[d - 1], er_sem.at[d - 1])
-        total = total + unpack(h2r[d - 1], hrows)
+        total = total + unpack(h2r[d - 1], hlong, WIDE)
+    total = unfold(total, hrows)
     high, low = split(total)
     parent = dot(high[:share], near[:, :width]) + dot(low[:share], near[:, :width])
     both = dot(high[share:], near) + dot(low[share:], near)
@@ -238,20 +261,7 @@
     gc[pl.ds(c, 1)] = gt[pl.ds(place, 1)]
 
     for e in range(1, ratio):
-        panels_arrive(e)
-    for e in range(nr):
-        value = q[e]
-        for d in range(1, ratio):
-            arrived(mx.at[d - 1, e], ms_sem.at[d - 1, e], mr_sem.at[d - 1, e])
-            half = lax.rem(x - d + ratio, ratio)
-            value = value + dot(mx[d - 1, e], jz[pl.ds(pl.multiple_of(half * cols, cols), cols), :])
-        if e < nr - 1:
-            zq[e] = pack(value)
-            to = lax.rem(z + 1 + e, nr) * ratio + x
-            start(zq.at[e], zrq.at[e], zs_sem.at[e], zr_sem.at[e], r, to)
-        else:
-            q[e] = value
-
+        panels_forward(e)
     for d in range(1, nc):
         come = lax.rem(c + nc - d, nc)
         arrived(gc.at[come], bs_sem.at[d - 1], br_sem.at[d - 1])
@@ -263,6 +273,32 @@
         for d in range(1, nc):
             to = lax.rem(c + d, nc)
             start(gf.at[r, c], gf.at[r, c], cs_sem.at[d - 1], cr_sem.at[d - 1], r, to)
+
+    for e in range(1, ratio):
+        panels_arrive(e)
+
+    def send_rows(value, i, to):
+        zq[i] = pack(value, WIDE)
+        start(zq.at[i], zrq.at[i], zs_sem.at[i], zr_sem.at[i], r, to * ratio + x)
+
+    for e in range(nr):
+        value = q[e]
+        for d in range(1, ratio):
+            arrived(mx.at[d - 1, e], ms_sem.at[d - 1, e], mr_sem.at[d - 1, e])
+            other = lax.rem(x - d + ratio, ratio)
+            value = value + dot(mx[d - 1, e], jz[pl.ds(pl.multiple_of(other * cols, cols), cols), :])
+        if e < half - 1:
+            send_rows(fold(value), e, pair_dest(0, 1 - side))
+        elif e == nr - 2:
+            send_rows(fold(value), half - 1, pair_dest(0, 1 - side))
+        else:
+            q[e] = value
+    for m in range(1, half):
+        arrived(zrq.at[m - 1], zs_sem.at[m - 1], zr_sem.at[m - 1])
+        value = fold(q[half + m - 2]) + unpack(zrq[m - 1], zlong, WIDE)
+        send_rows(value, half + m - 1, pair_dest(m, side))
+
+    if not shared:
         for d in range(1, nc):
             come = lax.rem(c + nc - d, nc)
             arrived(gf.at[r, come], cs_sem.at[d - 1], cr_sem.at[d - 1])
@@ -275,11 +311,11 @@
         arrived(gf.at[come], ds_sem.at[d - 1], dr_sem.at[d - 1])
         start(gf.at[come], gf.at[come], xs_sem.at[d], xr_sem.at[d], mate, c)
 
-    value = q[nr - 1]
-    for e in range(nr - 1):
-        arrived(zrq.at[e], zs_sem.at[e], zr_sem.at[e])
-        value = value + unpack(zrq[e], kr)
-    sum_ref[...] = value
+    value = fold(q[nr - 1])
+    for i in range(half - 1, nr - 1):
+        arrived(zrq.at[i], zs_sem.at[i], zr_sem.at[i])
+        value = value + unpack(zrq[i], zlong, WIDE)
+    sum_ref[...] = unfold(value, kr)
 
     for d in range(chips):
         come = lax.rem(chip + chips - d, chips) * 2 + 1 - core
@@ -348,6 +384,7 @@
     column = jax.ShapeDtypeStruct((kr, width), F32)
     others = max(ratio - 1, 1)
     chips, hrows = nr // 2, 2 * width // nr
+    hlong, zlong = hrows * cols // BLOCK, kr * 2 * width // BLOCK
     I16 = jnp.int16
     summed, small_sums = pl.pallas_call(
         functools.partial(kernel, nr, nc, lots),
@@ -365,13 +402,13 @@
             pltpu.VMEM((rows, 2 * width), BF16),
             pltpu.VMEM((others, nr, kr, cols), BF16),
             pltpu.VMEM((nr, kr, 2 * width), F32),
-            pltpu.VMEM((nr - 1, packed(kr), 2 * width), I16),
-            pltpu.VMEM((nr - 1, packed(kr), 2 * width), I16),
+            pltpu.VMEM((nr - 1, packed(zlong, WIDE), BLOCK), I16),
+            pltpu.VMEM((nr - 1, packed(zlong, WIDE), BLOCK), I16),
             pltpu.VMEM((2 * width, cols), F32),
-            pltpu.VMEM((chips, packed(hrows), cols), I16),
-            pltpu.VMEM((chips, packed(hrows), cols), I16),
-            pltpu.VMEM((chips - 1, packed(hrows), cols), I16),
-            pltpu.VMEM((chips - 1, packed(hrows), cols), I16),
+            pltpu.VMEM((chips, packed(hlong, WIDE), BLOCK), I16),
+            pltpu.VMEM((chips, packed(hlong, WIDE), BLOCK), I16),
+            pltpu.VMEM((chips - 1, packed(hlong, WIDE), BLOCK), I16),
+            pltpu.VMEM((chips - 1, packed(hlong, WIDE), BLOCK), I16),
             pltpu.VMEM((lots, packed(gcols), BLOCK), I16),
             pltpu.VMEM((nc, packed(gcols), BLOCK), I16),
             pltpu.VMEM((nr, lots, packed(gcols), BLOCK), I16),

time: 46.7 us -> 39.1 us (0.84)
  the two profiles are of different devices: /device:TPU:5 before, /device:TPU:0 now
where the time goes in v5:
time: 39.1 us; the launch traced here: 39 us
  Pallas kernels  38.3 us (98%)
  between operations  0.67 us (2%)
    pallas_call x1, Pallas kernels, shards(): pl.pallas_call(functools.partial(kernel, nr, nc, lots), out_shape=(pltpu....  37 us
    pallas_call x1, Pallas kernels, shards(): pl.pallas_call(finish, out_shape=(column, square, square, column, square)...  1.27 us

profile of v5, /device:TPU:0, one launch (start us, length us, event | category | flops | bytes accessed | tf_op | source)
XLA Modules:
  0.0 39.0 jit_solution(6031018470902483851)
XLA Ops:
  0.6 0.0 copy-start
  0.6 0.0 copy-start.1
  0.7 37.0 %shard_map.101 = (f32[128,512]{1,0:T(8,128)S(1)}, f32[1536,128]{1,0:T(8,128)S(1)}) custom-call(bf16[1024,512]{1,0:T(8,128)(2,1)} %m_any.1, s32[4,8]{1,0:T(4,128)} %bitcast.1, bf16[2,1024,256]{2,1,0:T(8,128)(2,1)} %f_any.1, s32[2,8]{1,0:T(2,128)} %pm_any.1), custom_call_target="tpu_custom_call" | custom-call | tf_op jit(solution)/shard_map/pallas_call | solution.py:389
  37.7 0.0 copy-done
  37.7 0.0 copy-done.1
  37.7 1.3 %shard_map.102 = (f32[128,256]{1,0:T(8,128)}, f32[256,256]{1,0:T(8,128)}, f32[256,256]{1,0:T(8,128)}, f32[128,256]{1,0:T(8,128)}, f32[256,256]{1,0:T(8,128)}) custom-call(f32[128,512]{1,0:T(8,128)S(1)} %get-tuple-element.7.sum_ref, f32[1536,128]{1,0:T(8,128)S(1)} %get-tuple-element.8.g_ref, bf16[256,256]{1,0:T(8,128)(2,1)S(1)} %copy-done.1, ...), custom_call_target="tpu_custom_call" | custom-call | tf_op jit(solution)/shard_map/pallas_call | solution.py:427
Async XLA Ops:
  0.6 37.0 %copy-start = (f32[2,256,256]{2,1,0:T(8,128)S(1)}, f32[2,256,256]{2,1,0:T(8,128)}, u32[]{:S(2)}) copy-start(f32[2,256,256]{2,1,0:T(8,128)} %piv_ref.1) | copy-start | bytes 1572868
  0.6 37.0 %copy-start.1 = (bf16[256,256]{1,0:T(8,128)(2,1)S(1)}, bf16[256,256]{1,0:T(8,128)(2,1)}, u32[]{:S(2)}) copy-start(bf16[256,256]{1,0:T(8,128)(2,1)} %top_ref.1) | copy-start | bytes 393220

commit v6 on v5

--- a/solution.py
+++ b/solution.py
@@ -293,11 +293,6 @@
             send_rows(fold(value), half - 1, pair_dest(0, 1 - side))
         else:
             q[e] = value
-    for m in range(1, half):
-        arrived(zrq.at[m - 1], zs_sem.at[m - 1], zr_sem.at[m - 1])
-        value = fold(q[half + m - 2]) + unpack(zrq[m - 1], zlong, WIDE)
-        send_rows(value, half + m - 1, pair_dest(m, side))
-
     if not shared:
         for d in range(1, nc):
             come = lax.rem(c + nc - d, nc)
@@ -306,10 +301,23 @@
         to = lax.rem(chip + d, chips) * 2 + core
         start(gf.at[r], gf.at[r], ds_sem.at[d - 1], dr_sem.at[d - 1], to, c)
     start(gf.at[r], gf.at[r], xs_sem.at[0], xr_sem.at[0], mate, c)
+    def restore(line):
+        block = jnp.concatenate([unpack(gf[line, j], gcols) for j in range(lots)], axis=0)
+        for k in range(3 * slots):
+            place_of = pl.multiple_of(k * width + line * share, 16)
+            g_ref[pl.ds(place_of, share), :] = block[k * share : (k + 1) * share, :]
+
+    restore(r)
+    for m in range(1, half):
+        arrived(zrq.at[m - 1], zs_sem.at[m - 1], zr_sem.at[m - 1])
+        value = fold(q[half + m - 2]) + unpack(zrq[m - 1], zlong, WIDE)
+        send_rows(value, half + m - 1, pair_dest(m, side))
+
     for d in range(1, chips):
         come = lax.rem(chip + chips - d, chips) * 2 + core
         arrived(gf.at[come], ds_sem.at[d - 1], dr_sem.at[d - 1])
         start(gf.at[come], gf.at[come], xs_sem.at[d], xr_sem.at[d], mate, c)
+        restore(come)
 
     value = fold(q[nr - 1])
     for i in range(half - 1, nr - 1):
@@ -320,10 +328,7 @@
     for d in range(chips):
         come = lax.rem(chip + chips - d, chips) * 2 + 1 - core
         arrived(gf.at[come], xs_sem.at[d], xr_sem.at[d])
-    for i in range(nr):
-        block = jnp.concatenate([unpack(gf[i, j], gcols) for j in range(lots)], axis=0)
-        for k in range(3 * slots):
-            g_ref[k * width + i * share : k * width + (i + 1) * share, :] = block[k * share : (k + 1) * share, :]
+        restore(come)
 
     for made in sent:
         made.wait_send()

time: 39.1 us -> 39.1 us (level)
  no operation moved by 1% of the time
where the time goes in v6:
time: 39.1 us; the launch traced here: 38.9 us
  Pallas kernels  38.2 us (98%)
  between operations  0.67 us (2%)
    pallas_call x1, Pallas kernels, shards(): pl.pallas_call(functools.partial(kernel, nr, nc, lots), out_shape=(pltpu....  37 us
    pallas_call x1, Pallas kernels, shards(): pl.pallas_call(finish, out_shape=(column, square, square, column, square)...  1.27 us

profile of v6, /device:TPU:0, one launch (start us, length us, event | category | flops | bytes accessed | tf_op | source)
XLA Modules:
  0.0 38.9 jit_solution(12569996136777667717)
XLA Ops:
  0.6 0.0 copy-start
  0.6 0.0 copy-start.1
  0.7 37.0 %shard_map.101 = (f32[128,512]{1,0:T(8,128)S(1)}, f32[1536,128]{1,0:T(8,128)S(1)}) custom-call(bf16[1024,512]{1,0:T(8,128)(2,1)} %m_any.1, s32[4,8]{1,0:T(4,128)} %bitcast.1, bf16[2,1024,256]{2,1,0:T(8,128)(2,1)} %f_any.1, s32[2,8]{1,0:T(2,128)} %pm_any.1), custom_call_target="tpu_custom_call" | custom-call | tf_op jit(solution)/shard_map/pallas_call | solution.py:394
  37.6 0.0 copy-done
  37.6 0.0 copy-done.1
  37.6 1.3 %shard_map.102 = (f32[128,256]{1,0:T(8,128)}, f32[256,256]{1,0:T(8,128)}, f32[256,256]{1,0:T(8,128)}, f32[128,256]{1,0:T(8,128)}, f32[256,256]{1,0:T(8,128)}) custom-call(f32[128,512]{1,0:T(8,128)S(1)} %get-tuple-element.7.sum_ref, f32[1536,128]{1,0:T(8,128)S(1)} %get-tuple-element.8.g_ref, bf16[256,256]{1,0:T(8,128)(2,1)S(1)} %copy-done.1, ...), custom_call_target="tpu_custom_call" | custom-call | tf_op jit(solution)/shard_map/pallas_call | solution.py:432
Async XLA Ops:
  0.6 37.0 %copy-start = (f32[2,256,256]{2,1,0:T(8,128)S(1)}, f32[2,256,256]{2,1,0:T(8,128)}, u32[]{:S(2)}) copy-start(f32[2,256,256]{2,1,0:T(8,128)} %piv_ref.1) | copy-start | bytes 1572868
  0.6 37.0 %copy-start.1 = (bf16[256,256]{1,0:T(8,128)(2,1)S(1)}, bf16[256,256]{1,0:T(8,128)(2,1)}, u32[]{:S(2)}) copy-start(bf16[256,256]{1,0:T(8,128)(2,1)} %top_ref.1) | copy-start | bytes 393220

commit v7 on v6

--- a/solution.py
+++ b/solution.py
@@ -185,8 +185,9 @@
 
     @pl.when(is_source)
     def _():
-        for made in panel_copies(0):
-            made.start()
+        for e in range(ratio):
+            for made in panel_copies(e):
+                made.start()
 
     loads[2].wait()
     loads[3].wait()
@@ -226,11 +227,6 @@
     @pl.when(is_source)
     def _():
         jz[...] = jown[...]
-        for made in panel_copies(0):
-            made.wait_send()
-        for e in range(1, ratio):
-            for made in panel_copies(e):
-                made.start()
 
     total = chunk(r) + unpack(h1r[chip], hlong, WIDE)
 
@@ -335,7 +331,7 @@
 
     @pl.when(is_source)
     def _():
-        for e in range(1, ratio):
+        for e in range(ratio):
             for made in panel_copies(e):
                 made.wait_send()
 

time: 39.1 us -> 41.6 us (1.064)
  Pallas kernels: 38.2 us -> 40.8 us
    pallas_call x1, Pallas kernels: 37 us -> 39.5 us  [shards(): pl.pallas_call(functools.partial(kernel, nr, nc, lots), out_shape=(pltpu....]
where the time goes in v7:
time: 41.6 us; the launch traced here: 41.5 us
  Pallas kernels  40.8 us (98%)
  between operations  0.67 us (2%)
    pallas_call x1, Pallas kernels, shards(): pl.pallas_call(functools.partial(kernel, nr, nc, lots), out_shape=(pltpu....  39.5 us
    pallas_call x1, Pallas kernels, shards(): pl.pallas_call(finish, out_shape=(column, square, square, column, square)...  1.27 us

profile of v7, /device:TPU:0, one launch (start us, length us, event | category | flops | bytes accessed | tf_op | source)
XLA Modules:
  0.0 41.5 jit_solution(15109442700016792559)
XLA Ops:
  0.6 0.0 copy-start
  0.6 0.0 copy-start.1
  0.7 39.5 %shard_map.101 = (f32[128,512]{1,0:T(8,128)S(1)}, f32[1536,128]{1,0:T(8,128)S(1)}) custom-call(bf16[1024,512]{1,0:T(8,128)(2,1)} %m_any.1, s32[4,8]{1,0:T(4,128)} %bitcast.1, bf16[2,1024,256]{2,1,0:T(8,128)(2,1)} %f_any.1, s32[2,8]{1,0:T(2,128)} %pm_any.1), custom_call_target="tpu_custom_call" | custom-call | tf_op jit(solution)/shard_map/pallas_call | solution.py:390
  40.2 0.0 copy-done
  40.2 0.0 copy-done.1
  40.2 1.3 %shard_map.102 = (f32[128,256]{1,0:T(8,128)}, f32[256,256]{1,0:T(8,128)}, f32[256,256]{1,0:T(8,128)}, f32[128,256]{1,0:T(8,128)}, f32[256,256]{1,0:T(8,128)}) custom-call(f32[128,512]{1,0:T(8,128)S(1)} %get-tuple-element.7.sum_ref, f32[1536,128]{1,0:T(8,128)S(1)} %get-tuple-element.8.g_ref, bf16[256,256]{1,0:T(8,128)(2,1)S(1)} %copy-done.1, ...), custom_call_target="tpu_custom_call" | custom-call | tf_op jit(solution)/shard_map/pallas_call | solution.py:428
Async XLA Ops:
  0.6 39.5 %copy-start = (f32[2,256,256]{2,1,0:T(8,128)S(1)}, f32[2,256,256]{2,1,0:T(8,128)}, u32[]{:S(2)}) copy-start(f32[2,256,256]{2,1,0:T(8,128)} %piv_ref.1) | copy-start | bytes 1572868
  0.6 39.5 %copy-start.1 = (bf16[256,256]{1,0:T(8,128)(2,1)S(1)}, bf16[256,256]{1,0:T(8,128)(2,1)}, u32[]{:S(2)}) copy-start(bf16[256,256]{1,0:T(8,128)(2,1)} %top_ref.1) | copy-start | bytes 393220
